TPU v7x, 256 devices: a whole 4x4x8 slice. The times are simulated.
256 devices in a mesh: replica: 32 (over y, x, core), tp: 8 (over z).
Axes of the slice: x: 4, y: 4, z: 8, core: 2. Of those that a mesh axis runs over, the one named last changes fastest.
Arguments:
- features: bfloat16 [2, 1024, 8192], P(None, 'replica', 'tp'), may hold values from -6 to 6
- gain: bfloat16 [8192], P('tp'), may hold values from 0.25 to 1.75
- w_key: bfloat16 [8192, 1024], P(None, 'tp'), may hold values from -0.0625 to 0.0625
- w_value: bfloat16 [8192, 1024], P(None, 'tp'), may hold values from -0.0625 to 0.0625
- pool_a: bfloat16 [1024, 8192, 64], P('replica', 'tp'), may hold values from -0.0625 to 0.0625
- pool_b: bfloat16 [1024, 64, 1024], P('replica', None, 'tp'), may hold values from -0.75 to 0.75
- placement: int32 [1024], replicated, may hold values from 0 to 1023, as said below
- need_lists: int32 [32, 16], replicated, may hold values from 0 to 1023, as said below
- row_adapter: int32 [1024], P('replica'), may hold values from 0 to 47, as said below
- lengths: int32 [1024], P('replica'), may hold values from 2 to 192, as said below
- queries: bfloat16 [2, 1024, 8192], P(None, 'replica', 'tp'), may hold values from -256 to 256
- cache_k: bfloat16 [1024, 192, 1024], P('replica', None, 'tp'), may hold values from -6 to 6
- cache_v: bfloat16 [1024, 192, 1024], P('replica', None, 'tp'), may hold values from -6 to 6
Outputs:
- attention: bfloat16 [2, 1024, 8192], P(None, 'replica', 'tp')
- new_keys: bfloat16 [2, 1024, 1024], P(None, 'replica', 'tp')
- new_values: bfloat16 [2, 1024, 1024], P(None, 'replica', 'tp')
Inputs may be any that keep to these rules, and one draw needn't show every extreme that they name: A permutation: adapter a sits in entry placement[a] % 32 of the pool of replica placement[a] // 32. `need_lists`: replica r's list names 16 different adapters stored on replicas other than r; at most 1 of them on one replica, exactly 1 on some. `row_adapter`: every entry below 16 is used by 1 to 2 rows of the replica, some by exactly 2. `lengths`: some row has exactly 192.
All inputs are finite; a program needn't handle non-finite values.
Results may differ from a plain program's by a relative error of at most 0.0056.
Values may be sent and summed in bfloat16 or wider, within the bound.
A program may use at most 128 MiB of HBM per device.

v0:
```python
import math

import jax
import jax.numpy as jnp
from jax import lax
from jax.sharding import PartitionSpec as P

HD = 128
GROUP = 8


eps = 1e-05
theta = 500000.0


def rotate(key_heads, positions):
    half_size = HD // 2
    frequency = theta ** (-(jnp.arange(half_size, dtype=jnp.float32) * 2.0) / HD)
    angles = positions.astype(jnp.float32)[:, None] * frequency[None, :]
    cosines = jnp.cos(angles)[:, None, :]
    sines = jnp.sin(angles)[:, None, :]
    front_half = key_heads[..., :half_size]
    back_half = key_heads[..., half_size:]
    return jnp.concatenate(
        [front_half * cosines - back_half * sines, back_half * cosines + front_half * sines],
        axis=-1,
    )


def attend(query_heads, cache_keys, cache_values, lengths, fresh_keys, fresh_values):
    score_scale = 1.0 / math.sqrt(HD)
    cached = (
        jnp.einsum("rkgd,rckd->rkgc", query_heads, cache_keys, preferred_element_type=jnp.float32)
        * score_scale
    )
    fresh_scores = (
        jnp.einsum("rkgd,nrkd->rkgn", query_heads, fresh_keys, preferred_element_type=jnp.float32)
        * score_scale
    )
    live_mask = jnp.arange(cache_keys.shape[1], dtype=jnp.int32)[None, :] < lengths[:, None]
    cached = jnp.where(live_mask[:, None, None, :], cached, -1e30)
    row_max = jnp.maximum(
        jnp.max(cached, axis=-1, keepdims=True), jnp.max(fresh_scores, axis=-1, keepdims=True)
    )
    cache_exp = jnp.exp(cached - row_max)
    fresh_exp = jnp.exp(fresh_scores - row_max)
    denominator = jnp.sum(cache_exp, axis=-1, keepdims=True) + jnp.sum(
        fresh_exp, axis=-1, keepdims=True
    )
    cache_weights = (cache_exp / denominator).astype(jnp.bfloat16)
    fresh_weights = (fresh_exp / denominator).astype(jnp.bfloat16)
    mixed = jnp.einsum(
        "rkgc,rckd->rkgd", cache_weights, cache_values, preferred_element_type=jnp.float32
    )
    return mixed + jnp.einsum(
        "rkgn,nrkd->rkgd", fresh_weights, fresh_values, preferred_element_type=jnp.float32
    )


def lookup(table, index):
    hits = index[..., None] == jnp.arange(table.shape[0], dtype=jnp.int32)
    return jnp.sum(jnp.where(hits, table, 0), axis=-1)


def earlier_count(labels):
    positions = labels.shape[-1]
    before_mask = jnp.arange(positions)[:, None] > jnp.arange(positions)[None, :]
    same_label = labels[..., :, None] == labels[..., None, :]
    return jnp.sum(jnp.where(before_mask & same_label, 1, 0), axis=-1).astype(jnp.int32)


def low_rank(own_normed, down_rows, up_rows):
    partial_sum = jnp.einsum(
        "srd,rdk->srk", own_normed, down_rows, preferred_element_type=jnp.float32
    )
    lowrank = lax.psum(partial_sum, "tp")
    coeff = lowrank.astype(jnp.bfloat16)
    return jnp.einsum("srk,rkc->src", coeff, up_rows, preferred_element_type=jnp.float32)


def shards(
    features,
    gain,
    w_key,
    w_value,
    pool_a,
    pool_b,
    placement,
    need_lists,
    row_adapter,
    lengths,
    queries,
    cache_k,
    cache_v,
):
    step_count, row_count, slice_width = features.shape
    head_cols = w_key.shape[1]
    kv_local = head_cols // HD
    pool_size = pool_a.shape[0]
    cache_len = cache_k.shape[1]
    need_count = need_lists.shape[1]
    replicas = lax.axis_size("replica")
    capacity = (need_count + replicas - 2) // (replicas - 1)
    replica_index = lax.axis_index("replica")
    tp_index = lax.axis_index("tp")
    whole_rows, gain_whole = (
        lax.all_gather(features, "tp", axis=2, tiled=True),
        lax.all_gather(gain.reshape(1, 1, slice_width), "tp", axis=2, tiled=True),
    )
    values = whole_rows.astype(jnp.float32)
    scaled = (
        values
        * lax.rsqrt(jnp.mean(values * values, axis=-1, keepdims=True) + eps)
        * gain_whole.astype(jnp.float32)
    )
    hidden = scaled.astype(jnp.bfloat16)
    own_normed = lax.dynamic_slice_in_dim(hidden, tp_index * slice_width, slice_width, 2)
    key_base = jnp.einsum("srd,dc->src", hidden, w_key, preferred_element_type=jnp.float32)
    value_base = jnp.einsum("srd,dc->src", hidden, w_value, preferred_element_type=jnp.float32)
    listed = lax.dynamic_index_in_dim(need_lists, replica_index, 0, keepdims=False)
    listed_slot = lookup(placement, listed)
    listed_turn = earlier_count(listed_slot // pool_size)
    menu_hit = row_adapter[:, None] == jnp.arange(need_count, dtype=jnp.int32)[None, :]
    remote = row_adapter < need_count
    far_slot = jnp.sum(jnp.where(menu_hit, listed_slot[None, :], 0), axis=1)
    row_owner = jnp.where(remote, far_slot // pool_size, replica_index)
    row_local = jnp.where(remote, far_slot % pool_size, row_adapter - need_count)
    row_turn = jnp.sum(jnp.where(menu_hit, listed_turn[None, :], 0), axis=1)
    near_down = pool_a[row_local]
    near_up = pool_b[row_local]
    every_slot = lookup(placement, need_lists)
    every_owner = every_slot // pool_size
    every_local = every_slot % pool_size
    every_turn = earlier_count(every_owner)
    wanted = (every_owner == replica_index)[:, :, None] & (
        every_turn[:, :, None] == jnp.arange(capacity, dtype=jnp.int32)[None, None, :]
    )
    send_index = jnp.sum(jnp.where(wanted, every_local[:, :, None], 0), axis=1)
    fetched_down, fetched_up = (
        lax.all_to_all(pool_a[send_index], "replica", split_axis=0, concat_axis=0, tiled=True),
        lax.all_to_all(pool_b[send_index], "replica", split_axis=0, concat_axis=0, tiled=True),
    )
    far_index = row_owner * capacity + row_turn
    far_down = fetched_down.reshape(replicas * capacity, slice_width, -1)[far_index]
    far_up = fetched_up.reshape(replicas * capacity, -1, head_cols)[far_index]
    down_rows = jnp.where(remote[:, None, None], far_down, near_down)
    up_rows = jnp.where(remote[:, None, None], far_up, near_up)
    delta = low_rank(own_normed, down_rows, up_rows)
    new_values = (value_base + delta).astype(jnp.bfloat16)
    cache_keys = cache_k.reshape(row_count, cache_len, kv_local, HD)
    cache_values = cache_v.reshape(row_count, cache_len, kv_local, HD)
    key_list = []
    attention = []
    for which_step in range(step_count):
        rotated = rotate(
            key_base[which_step].reshape(row_count, kv_local, HD), lengths + which_step
        )
        key_list.append(rotated.reshape(row_count, head_cols).astype(jnp.bfloat16))
        fresh_keys = jnp.stack(key_list).reshape(which_step + 1, row_count, kv_local, HD)
        fresh_values = new_values[: which_step + 1].reshape(which_step + 1, row_count, kv_local, HD)
        query_heads = queries[which_step].reshape(row_count, kv_local, GROUP, HD)
        mixed = attend(query_heads, cache_keys, cache_values, lengths, fresh_keys, fresh_values)
        attention.append(mixed.reshape(row_count, kv_local * GROUP * HD).astype(jnp.bfloat16))
    return (jnp.stack(attention), jnp.stack(key_list), new_values)


def solution(mesh):
    placed = (
        P(None, "replica", "tp"),
        P("tp"),
        P(None, "tp"),
        P(None, "tp"),
        P("replica", "tp", None),
        P("replica", None, "tp"),
        P(),
        P(),
        P("replica"),
        P("replica"),
        P(None, "replica", "tp"),
        P("replica", None, "tp"),
        P("replica", None, "tp"),
    )
    return jax.shard_map(
        shards,
        mesh=mesh,
        in_specs=placed,
        out_specs=(P(None, "replica", "tp"), P(None, "replica", "tp"), P(None, "replica", "tp")),
        check_vma=False,
    )
```

profile of v0, /device:TPU:0, one launch (start us, length us, event | category | flops | bytes accessed | tf_op | source)
XLA Modules:
  0.0 180.1 jit_solution(4265551597877059424)
XLA Ops:
  7.3 0.7 all-gather.3.cloned.1.call-update
  8.0 0.8 copy.44
  8.8 1.4 select_reduce_fusion
  10.6 2.5 %gather_fusion = bf16[32,64,128]{2,1,0:T(8,128)(2,1)} fusion(bf16[32,64,128]{2,1,0:T(8,128)(2,1)} %param.18, s32[1024]{0:T(1024)S(1)} %pad_clamp_fusion.2), kind=kCustom, calls=%fused_computation | custom fusion | bytes 1048704 | tf_op jit(solution)/shard_map/gather | solution.py:141
  13.1 5.6 %all-to-all-start = ((bf16[32,1,64,128]{3,2,1,0:T(8,128)(2,1)}), bf16[32,1,64,128]{3,2,1,0:T(8,128)(2,1)S(1)}, u32[]{:S(2)}, u32[]{:S(2)}) async-start(bf16[32,1,64,128]{3,2,1,0:T(8,128)(2,1)} %bitcast.9), calls=%async_computation | async-start | bytes 1048576 | tf_op jit(solution)/shard_map/all_to_all | solution.py:141
  19.6 0.6 broadcast_compare_fusion
  20.2 3.6 %fusion.69 = (f32[32,8]{1,0:T(8,128)}, f32[32,8,192]{2,1,0:T(8,128)}) fusion(bf16[32,8,128]{2,1,0:T(8,128)(2,1)S(1)} %bitcast.63, bf16[32,192,128]{2,1,0:T(8,128)(2,1)} %param.24, pred[32,192]{1,0:T(8,128)(4,1)S(1)} %iota_compare_fusion.2), kind=kOutput, calls=%fused_computation.136 | convolution fusion | flops 12730112 | bytes 1842176 | tf_op jit(solution)/shard_map/rkgd,rckd->rkgc/dot_general | solution.py:33
  23.9 0.6 multiply_power_fusion
  24.5 5.0 %gather_fusion.3 = bf16[32,1024,64]{1,2,0:T(8,128)(2,1)} fusion(bf16[32,1024,64]{1,2,0:T(8,128)(2,1)} %param.17, s32[1024]{0:T(1024)S(1)} %pad_clamp_fusion.2), kind=kCustom, calls=%fused_computation.3 | custom fusion | bytes 8388736 | tf_op jit(solution)/shard_map/gather | solution.py:140
  29.5 5.0 %gather_fusion.5 = bf16[32,1024,64]{1,2,0:T(8,128)(2,1)} fusion(bf16[32,1024,64]{1,2,0:T(8,128)(2,1)} %param.17, s32[1024]{0:T(1024)S(1)} %get-tuple-element.25), kind=kCustom, calls=%fused_computation.5 | custom fusion | bytes 8388736 | tf_op jit(solution)/shard_map/gather | solution.py:129
  34.5 1.4 gather_fusion.2
  35.8 25.4 %all-gather = bf16[8192]{0:T(1024)(128)(2,1)S(1)} all-gather(bf16[1024]{0:T(1024)(128)(2,1)S(1)} %copy-done.22), channel_id=2, replica_groups=mesh['replica'=32,'tp'=8] {'tp'}, dimensions={0}, use_global_device_ids=true | all-gather | bytes 18432 | tf_op jit(solution)/shard_map/all_gather | solution.py:108
  61.3 0.6 mul.164
  61.9 0.6 fusion.66
  62.5 3.0 %fusion.67 = (f32[32,8]{1,0:T(8,128)}, f32[32,8,192]{2,1,0:T(8,128)S(1)}) fusion(bf16[32,8,128]{2,1,0:T(8,128)(2,1)S(1)} %bitcast.65, bf16[32,192,128]{2,1,0:T(8,128)(2,1)} %param.24, pred[32,192]{1,0:T(8,128)(4,1)S(1)} %iota_compare_fusion.2), kind=kOutput, calls=%fused_computation.134 | convolution fusion | flops 12730112 | bytes 1842176 | tf_op jit(solution)/shard_map/rkgd,rckd->rkgc/dot_general | solution.py:33
  65.5 7.5 %all-to-all-start.1 = ((bf16[32,1,1024,64]{2,3,1,0:T(8,128)(2,1)}), bf16[32,1,1024,64]{2,3,1,0:T(8,128)(2,1)}, u32[]{:S(2)}, u32[]{:S(2)}) async-start(bf16[32,1,1024,64]{2,3,1,0:T(8,128)(2,1)} %bitcast.61), calls=%async_computation.1 | async-start | bytes 8388608 | tf_op jit(solution)/shard_map/all_to_all | solution.py:140
  73.0 1.4 gather_fusion.1
  74.4 1.5 fusion.3
  76.0 1.5 fusion.5
  77.6 0.5 fusion.8
  79.5 0.6 add.131
  80.2 0.7 constant_dynamic-slice_fusion
  81.7 0.6 fusion.61
  82.3 44.2 %all-to-all-done.1 = bf16[32,1,1024,64]{2,3,1,0:T(8,128)(2,1)} async-done(((bf16[32,1,1024,64]{2,3,1,0:T(8,128)(2,1)}), bf16[32,1,1024,64]{2,3,1,0:T(8,128)(2,1)}, u32[]{:S(2)}, u32[]{:S(2)}) %all-to-all-start.1) | async-done | bytes 4194336 | tf_op jit(solution)/shard_map/all_to_all | solution.py:140
  126.5 5.1 %gather_fusion.4 = bf16[32,1024,64]{1,2,0:T(8,128)(2,1)} fusion(bf16[32,1024,64]{1,2,0:T(8,128)(2,1)} %bitcast.12, s32[1024]{0:T(1024)} %copy-done.20), kind=kCustom, calls=%fused_computation.4 | custom fusion | bytes 8388736 | tf_op jit(solution)/shard_map/gather | solution.py:144
  131.6 5.4 %fusion.17 = f32[2,32,64]{2,0,1:T(2,128)} fusion(bf16[32,1024,64]{1,2,0:T(8,128)(2,1)} %gather_fusion.4, bf16[32,1024,64]{1,2,0:T(8,128)(2,1)} %gather_fusion.5, pred[32]{0:T(512)(128)(4,1)} %broadcast_compare_fusion, bf16[2,32,1024]{2,1,0:T(8,128)(2,1)S(1)} %copy-done.7), kind=kOutput, calls=%fused_computation.29 | convolution fusion | flops 10485760 | bytes 8536096 | tf_op jit(solution)/shard_map/srd,rdk->srk/dot_general | solution.py:73
  137.0 28.9 %psum.7 = bf16[2,32,64]{2,0,1:T(2,128)(2,1)S(1)} all-reduce(f32[2,32,64]{2,0,1:T(2,128)} %fusion.17), channel_id=1, replica_groups=mesh['replica'=32,'tp'=8] {'tp'}, use_global_device_ids=true, to_apply=%region_10.11 | all-reduce | flops 4096 | bytes 24576 | tf_op jit(solution)/shard_map/psum | solution.py:76
  165.9 1.6 fusion.24
  167.6 2.1 %fusion.21 = bf16[2,32,128]{2,1,0:T(8,128)(2,1)S(1)} fusion(bf16[2,32,8192]{2,1,0:T(8,128)(2,1)S(1)} %fusion.5, bf16[8192,128]{1,0:T(8,128)(2,1)} %param.16, f32[32,128,2]{1,2,0:T(2,128)S(1)} %fusion.24), kind=kOutput, calls=%fused_computation.32 | convolution fusion | flops 134234112 | bytes 3194880 | tf_op jit(solution)/shard_map/srd,dc->src/dot_general | solution.py:119
  169.7 0.6 fusion.12
  170.6 2.0 %fusion.13 = bf16[32,8,128]{2,1,0:T(8,128)(2,1)S(1)} fusion(f32[32,8,128]{2,1,0:T(8,128)S(1)} %fusion.43, bf16[32,192,128]{2,1,0:T(8,128)(2,1)} %param.25, f32[32,8,192]{2,1,0:T(8,128)S(1)} %get-tuple-element.20, f32[32,8]{1,0:T(8,128)S(1)} %copy-done.9, f32[32,8]{1,0:T(8,128)S(1)} %max.15), kind=kOutput, calls=%fused_computation.27 | convolution fusion | flops 12795904 | bytes 1968128 | tf_op jit(solution)/shard_map/rkgc,rckd->rkgd/dot_general | solution.py:52
  172.6 0.7 pad_maximum_fusion
  (95 shorter events, 4.0 us)
Async XLA Ops:
  7.2 70.4 %copy-start = (bf16[8192,128]{1,0:T(8,128)(2,1)S(1)}, bf16[8192,128]{1,0:T(8,128)(2,1)}, u32[]{:S(2)}) copy-start(bf16[8192,128]{1,0:T(8,128)(2,1)} %param.15) | copy-start | bytes 6291460
  7.2 11.5 %copy-start.13 = (s32[32,16]{0,1:T(8,128)S(1)}, s32[32,16]{0,1:T(8,128)}, u32[]{:S(2)}) copy-start(s32[32,16]{0,1:T(8,128)} %param.20) | copy-start | bytes 6148
  7.2 11.7 %copy-start.18 = (s32[1024]{0:T(1024)S(1)}, s32[1024]{0:T(1024)}, u32[]{:S(2)}) copy-start(s32[1024]{0:T(1024)} %param.19) | copy-start | bytes 12292
  7.2 11.9 %copy-start.6 = (bf16[2,32,1024]{2,1,0:T(8,128)(2,1)S(1)}, bf16[2,32,1024]{2,1,0:T(8,128)(2,1)}, u32[]{:S(2)}) copy-start(bf16[2,32,1024]{2,1,0:T(8,128)(2,1)} %param.23) | copy-start | bytes 393220
  7.2 12.1 %copy-start.23 = (s32[32]{0:T(128)S(1)}, s32[32]{0:T(128)}, u32[]{:S(2)}) copy-start(s32[32]{0:T(128)} %param.21) | copy-start | bytes 388
  7.2 12.9 %copy-start.26 = (s32[32]{0:T(128)S(1)}, s32[32]{0:T(128)}, u32[]{:S(2)}) copy-start(s32[32]{0:T(128)} %param.22) | copy-start | bytes 388
  7.2 67.2 %all-gather.3.cloned.1.call-start = ((), (), s32[]{:S(2)}) async-start(), calls=%async_computation.2 | async-start | bytes 1179648 | tf_op jit(solution)/shard_map/all_gather | solution.py:107
  13.1 52.4 %all-to-all-start = ((bf16[32,1,64,128]{3,2,1,0:T(8,128)(2,1)}), bf16[32,1,64,128]{3,2,1,0:T(8,128)(2,1)S(1)}, u32[]{:S(2)}, u32[]{:S(2)}) async-start(bf16[32,1,64,128]{3,2,1,0:T(8,128)(2,1)} %bitcast.9), calls=%async_computation | async-start | bytes 1048576 | tf_op jit(solution)/shard_map/all_to_all | solution.py:141
  19.6 53.4 %copy-start.20 = (s32[1024]{0:T(1024)}, s32[1024]{0:T(1024)S(1)}, u32[]{:S(2)}) copy-start(s32[1024]{0:T(1024)S(1)} %get-tuple-element.26) | copy-start | bytes 12292
  29.4 5.0 %copy-start.1 = (bf16[32,64,128]{2,1,0:T(8,128)(2,1)S(1)}, bf16[32,64,128]{2,1,0:T(8,128)(2,1)}, u32[]{:S(2)}) copy-start(bf16[32,64,128]{2,1,0:T(8,128)(2,1)} %param.18) | copy-start | bytes 1572868
  29.5 6.4 %copy-start.22 = (bf16[1024]{0:T(1024)(128)(2,1)S(1)}, bf16[1024]{0:T(1024)(128)(2,1)}, u32[]{:S(2)}) copy-start(bf16[1024]{0:T(1024)(128)(2,1)} %param.14) | copy-start | bytes 6148
  65.5 61.0 %all-to-all-start.1 = ((bf16[32,1,1024,64]{2,3,1,0:T(8,128)(2,1)}), bf16[32,1,1024,64]{2,3,1,0:T(8,128)(2,1)}, u32[]{:S(2)}, u32[]{:S(2)}) async-start(bf16[32,1,1024,64]{2,3,1,0:T(8,128)(2,1)} %bitcast.61), calls=%async_computation.1 | async-start | bytes 8388608 | tf_op jit(solution)/shard_map/all_to_all | solution.py:140
  77.5 0.7 copy-start.21
  77.5 0.7 copy-start.25
  77.6 0.9 copy-start.24
  77.6 1.3 copy-start.8
  77.6 3.5 %copy-start.5 = (f32[32,8]{1,0:T(8,128)S(1)}, f32[32,8]{1,0:T(8,128)}, u32[]{:S(2)}) copy-start(f32[32,8]{1,0:T(8,128)} %get-tuple-element.23) | copy-start | bytes 3076
  77.6 3.5 %copy-start.3 = (f32[32,8,192]{2,1,0:T(8,128)S(1)}, f32[32,8,192]{2,1,0:T(8,128)}, u32[]{:S(2)}) copy-start(f32[32,8,192]{2,1,0:T(8,128)} %get-tuple-element.24) | copy-start | bytes 589828
  78.7 0.6 copy-start.19
  78.9 2.4 %copy-start.14 = (f32[32,8,2]{1,2,0:T(2,128)}, f32[32,8,2]{1,2,0:T(2,128)S(1)}, u32[]{:S(2)}) copy-start(f32[32,8,2]{1,2,0:T(2,128)S(1)} %get-tuple-element.22) | copy-start | bytes 6148
  81.1 0.6 copy-start.10
  126.5 5.1 %copy-start.7 = (bf16[2,32,1024]{2,1,0:T(8,128)(2,1)S(1)}, bf16[2,32,1024]{2,1,0:T(8,128)(2,1)}, u32[]{:S(2)}) copy-start(bf16[2,32,1024]{2,1,0:T(8,128)(2,1)} %constant_dynamic-slice_fusion) | copy-start | bytes 393220
  165.9 3.8 %copy-start.2 = (bf16[32,192,128]{2,1,0:T(8,128)(2,1)S(1)}, bf16[32,192,128]{2,1,0:T(8,128)(2,1)}, u32[]{:S(2)}) copy-start(bf16[32,192,128]{2,1,0:T(8,128)(2,1)} %param.25) | copy-start | bytes 4718596
  165.9 3.8 %copy-start.4 = (f32[32,8,192]{2,1,0:T(8,128)S(1)}, f32[32,8,192]{2,1,0:T(8,128)}, u32[]{:S(2)}) copy-start(f32[32,8,192]{2,1,0:T(8,128)} %get-tuple-element.24) | copy-start | bytes 589828
  165.9 3.8 %copy-start.11 = (f32[32,8]{1,0:T(8,128)S(1)}, f32[32,8]{1,0:T(8,128)}, u32[]{:S(2)}) copy-start(f32[32,8]{1,0:T(8,128)} %copy-done.10) | copy-start | bytes 3076
  165.9 3.8 %copy-start.16 = (f32[32,8]{1,0:T(8,128)S(1)}, f32[32,8]{1,0:T(8,128)}, u32[]{:S(2)}) copy-start(f32[32,8]{1,0:T(8,128)} %get-tuple-element.7) | copy-start | bytes 3076
  165.9 3.8 %copy-start.17 = (f32[32,8]{1,0:T(8,128)S(1)}, f32[32,8]{1,0:T(8,128)}, u32[]{:S(2)}) copy-start(f32[32,8]{1,0:T(8,128)} %get-tuple-element.8) | copy-start | bytes 3076
  167.5 2.8 %copy-start.9 = (f32[32,8]{1,0:T(8,128)S(1)}, f32[32,8]{1,0:T(8,128)}, u32[]{:S(2)}) copy-start(f32[32,8]{1,0:T(8,128)} %add.131) | copy-start | bytes 3076
  167.5 2.8 %copy-start.15 = (f32[32,8,2]{1,2,0:T(2,128)S(1)}, f32[32,8,2]{1,2,0:T(2,128)}, u32[]{:S(2)}) copy-start(f32[32,8,2]{1,2,0:T(2,128)} %copy-done.14) | copy-start | bytes 6148
  169.7 2.9 %copy-start.12 = (bf16[2,32,128]{2,1,0:T(8,128)(2,1)}, bf16[2,32,128]{2,1,0:T(8,128)(2,1)S(1)}, u32[]{:S(2)}) copy-start(bf16[2,32,128]{2,1,0:T(8,128)(2,1)S(1)} %fusion.21) | copy-start | bytes 49156
Sparse Core Ops, SparseCore 0:
  9.9 39.9 all-gather.2
where the time goes:
time: 181 us; the launch traced here: 180 us
  blocking collectives  54.3 us (30%)
  waiting for transfers between devices  44.9 us (25%)
  local copies, waits for them, and re-layouts  23.3 us (13%)
  matrix products  19.3 us (11%)
  between operations  14.5 us (8%)
  starting transfers between devices  13.1 us (7%)
  other arithmetic  10.7 us (6%)
    all_to_all x1, waiting for transfers between devices, shards(): lax.all_to_all(pool_a[send_index], 'replica', split_axis=0, concat_axis=0...  44.2 us
    psum x1, blocking collectives, low_rank(): lowrank = lax.psum(partial_sum, 'tp')  28.9 us
    all_gather x1, blocking collectives, shards(): lax.all_gather(gain.reshape(1, 1, slice_width), 'tp', axis=2, tiled=True)  25.4 us
    all_to_all x1, starting transfers between devices, shards(): lax.all_to_all(pool_a[send_index], 'replica', split_axis=0, concat_axis=0...  7.49 us
    dot_general x2, matrix products, attend(): jnp.einsum('rkgd,rckd->rkgc', query_heads, cache_keys, preferred_element_...  6.66 us
    all_to_all x1, starting transfers between devices, shards(): lax.all_to_all(pool_b[send_index], 'replica', split_axis=0, concat_axis=0...  5.59 us
    dot_general x1, matrix products, low_rank(): jnp.einsum('srd,rdk->srk', own_normed, down_rows, preferred_element_type=...  5.35 us
    gather x1, local copies, waits for them, and re-layouts, shards(): fetched_down.reshape(replicas * capacity, slice_width, -1)[far_index]  5.13 us
  transfers between devices with their start and end apart: 3, of which 1 were waited for; matrix products, arithmetic and copies ran while one was open for 19% of the time, Pallas kernels for 0%

commit v1 on v0

v1 whole, which is shorter than its diff:
```python
import functools
import math

import jax
import jax.numpy as jnp
import numpy as np
from jax import lax
from jax.experimental import pallas as pl
from jax.experimental.pallas import tpu as pltpu
from jax.sharding import PartitionSpec as P

HD = 128
GROUP = 8
EPS = 1e-05
THETA = 500000.0
NEG = -1e30
MESH = pl.DeviceIdType.MESH
F32 = jnp.float32
BF16 = jnp.bfloat16
QUARTER = 256
NT = (((1,), (1,)), ((), ()))


def iota(shape, dim):
    return lax.broadcasted_iota(jnp.int32, shape, dim)


def kernel(
    nr,
    nt,
    f_ref,
    gain_ref,
    place_ref,
    need_ref,
    ra_ref,
    len_s,
    len_ref,
    freq_ref,
    q_ref,
    wk_hbm,
    wv_hbm,
    pa_hbm,
    pb_hbm,
    ck_hbm,
    cv_hbm,
    att_ref,
    nk_ref,
    nv_ref,
    wbuf,
    pa,
    pb,
    pbt,
    ck,
    cv,
    stats,
    msg,
    got,
    xall,
    ring,
    part,
    rs_got,
    coeff,
    expand,
    ret_send,
    ret_got,
    scores,
    weights,
    fresh_w,
    acc_kv,
    att_acc,
    load_sem,
    st_send,
    st_recv,
    a2a_send,
    a2a_recv,
    ring_send,
    ring_recv,
    rs_send,
    rs_recv,
    ag_send,
    ag_recv,
    re_send,
    re_recv,
):
    r = lax.axis_index("replica")
    t = lax.axis_index("tp")
    rows2, width = f_ref.shape
    rows = rows2 // 2
    need_count = need_ref.shape[0]
    adapters = place_ref.shape[1]
    pool = adapters // nr
    rank = part.shape[1] * nt
    kpart = rank // nt
    nvis = nr * 4
    ntot = nvis + rows2

    loads = [
        pltpu.make_async_copy(ck_hbm, ck, load_sem.at[0]),
        pltpu.make_async_copy(pa_hbm, pa, load_sem.at[1]),
        pltpu.make_async_copy(wk_hbm, wbuf.at[:, pl.ds(0, HD)], load_sem.at[2]),
        pltpu.make_async_copy(wv_hbm, wbuf.at[:, pl.ds(HD, HD)], load_sem.at[3]),
        pltpu.make_async_copy(pb_hbm, pb, load_sem.at[4]),
        pltpu.make_async_copy(cv_hbm, cv, load_sem.at[5]),
    ]
    for load in loads:
        load.start()

    barrier = pltpu.get_barrier_semaphore()

    @pl.loop(1, nr)
    def _(k):
        pl.semaphore_signal(
            barrier, inc=1, device_id=(lax.rem(r + k, nr), t), device_id_type=MESH
        )

    @pl.loop(1, nt)
    def _(k):
        pl.semaphore_signal(
            barrier, inc=1, device_id=(r, lax.rem(t + k, nt)), device_id_type=MESH
        )

    gain = gain_ref[...].astype(F32)
    f32 = f_ref[...].astype(F32)
    lanes = HD
    chunks = width // lanes
    eye = iota((rows2, lanes), 0) == iota((rows2, lanes), 1)
    square_sum = jnp.sum(f32 * f32, axis=1, keepdims=True)
    square_row = jnp.sum(jnp.where(eye, square_sum, 0.0), axis=0, keepdims=True)
    gain_rows = jnp.concatenate(
        [gain[:, c * lanes : (c + 1) * lanes] for c in range(chunks)], axis=0
    )
    stats[t] = jnp.concatenate(
        [gain_rows, jnp.broadcast_to(square_row, (8, lanes))], axis=0
    )
    own = (f32 * gain).astype(BF16)
    xall[pl.ds(nvis, rows2), :] = own

    ra = ra_ref[...]
    need = need_ref[...]
    mine = jnp.sum(
        jnp.where(iota(need.shape, 1) == r, need, 0).astype(F32), axis=1, keepdims=True
    )
    entry = iota((need_count, rows), 0) == ra
    wanted = jnp.sum(jnp.where(entry, mine, 0.0), axis=0, keepdims=True)
    place = place_ref[...]
    home = place // pool
    local = place - home * pool
    at_me = jnp.where(home == r, local + 1, 0)
    table = jnp.concatenate(
        [
            jnp.broadcast_to(x.astype(F32), (8, adapters))
            for x in (home, local, at_me)
        ],
        axis=0,
    ).astype(BF16)
    which = iota((adapters, rows), 0) == wanted.astype(jnp.int32)
    found = jnp.dot(
        table, jnp.where(which, 1.0, 0.0).astype(BF16), preferred_element_type=F32
    )
    owner = found[0:1].astype(jnp.int32)
    eye_r = iota((rows, rows), 0) == iota((rows, rows), 1)
    ra_f = ra.astype(F32)
    ra_col = jnp.sum(jnp.where(eye_r, ra_f, 0.0), axis=1, keepdims=True)
    twin = (ra_col == ra_f) & (iota((rows, rows), 0) < iota((rows, rows), 1))
    turn = jnp.sum(jnp.where(twin, 1.0, 0.0), axis=0, keepdims=True).astype(jnp.int32)
    is_far = ra < need_count
    code = jnp.where(is_far, owner * 16 + turn * 8, -1000)
    code2 = jnp.concatenate([code, code + 4], axis=1)

    slot_iota = iota((nr * 16, rows2), 0)
    total = None
    for j in range(4):
        pick = jnp.where(slot_iota == code2 + j, 1.0, 0.0).astype(BF16)
        piece = jnp.dot(
            pick, own[:, j * QUARTER : (j + 1) * QUARTER], preferred_element_type=F32
        )
        total = piece if total is None else total + piece
    msg[...] = total.astype(BF16)
    got[pl.ds(pl.multiple_of(r * 16, 16), 16), :] = jnp.zeros((16, QUARTER), BF16)
    ret_got[pl.ds(pl.multiple_of(r * 8, 8), 8), :] = jnp.zeros((8, HD), F32)

    pl.semaphore_wait(barrier, nr - 1 + nt - 1)

    right = (r, lax.rem(t + 1, nt))
    left = (r, lax.rem(t + nt - 1, nt))
    half = nt // 2

    def hop(which_way, h, c):
        if which_way == 0:
            have, there, to = (nt - (h - 1)) % nt, nt - h, right
        else:
            have, there, to = h - 1, h, left
        piece = pl.ds(c * rows, rows)
        src = f_ref.at[piece, :] if have == 0 else ring.at[have, piece, :]
        return pltpu.make_async_remote_copy(
            src_ref=src,
            dst_ref=ring.at[there, piece, :],
            send_sem=ring_send.at[which_way, h - 1, c],
            recv_sem=ring_recv.at[there, c],
            device_id=to,
            device_id_type=MESH,
        )

    def hops(h):
        if h < half:
            return [(0, 0), (1, 0), (0, 1), (1, 1)]
        return [(0, 0), (1, 1)]

    for way, c in hops(1):
        hop(way, 1, c).start()

    @pl.loop(1, nt)
    def _(k):
        pltpu.make_async_remote_copy(
            src_ref=stats.at[t],
            dst_ref=stats.at[t],
            send_sem=st_send,
            recv_sem=st_recv,
            device_id=(r, lax.rem(t + k, nt)),
            device_id_type=MESH,
        ).start()

    @pl.loop(1, nr)
    def _(k):
        to = lax.rem(r + k, nr)
        pltpu.make_async_remote_copy(
            src_ref=msg.at[pl.ds(pl.multiple_of(to * 16, 16), 16), :],
            dst_ref=got.at[pl.ds(pl.multiple_of(r * 16, 16), 16), :],
            send_sem=a2a_send,
            recv_sem=a2a_recv,
            device_id=(to, t),
            device_id_type=MESH,
        ).start()

    def wait_bytes(ref, sem):
        pltpu.make_async_copy(ref, ref, sem).wait()

    asked = jnp.zeros((adapters, nr), jnp.bool_)
    p_iota = iota((adapters, nr), 0)
    for e in range(need_count):
        asked = asked | (p_iota == need[e : e + 1, :])
    visit = jnp.dot(
        table, jnp.where(asked, 1.0, 0.0).astype(BF16), preferred_element_type=F32
    )[16:24]
    spread = jnp.where(iota((nr, nvis), 1) // 4 == iota((nr, nvis), 0), 1.0, 0.0)
    visit_slot = jnp.dot(
        visit.astype(BF16), spread.astype(BF16), preferred_element_type=F32
    )[0:1].astype(jnp.int32) - 1
    own_slot = jnp.where(is_far, -1, ra - need_count)
    slot_row = jnp.concatenate([visit_slot, own_slot, own_slot], axis=1)

    scale = 1.0 / math.sqrt(HD)
    cache_len = ck.shape[1]
    per_row = 2 * GROUP

    def cached_scores(lo, hi):
        @pl.loop(lo, hi, unroll=4)
        def _(i):
            s = (
                lax.dot_general(q_ref[i], ck[i], NT, preferred_element_type=F32) * scale
            )
            live = iota(s.shape, 1) < len_s[i]
            scores[i] = jnp.where(live, s, NEG)

    def ring_stage(h):
        for way, c in hops(h):
            hop(way, h, c).wait_recv()
            if (way, c) in (hops(h + 1) if h < half else []):
                hop(way, h + 1, c).start()

    loads[0].wait()
    cached_scores(0, rows // 2)
    ring_stage(1)

    loads[1].wait()
    wait_bytes(got.at[pl.ds(0, (nr - 1) * 16), :], a2a_recv)
    arrived = got[...]
    for j in range(4):
        gather = iota((nvis, nr * 16), 1) == iota((nvis, nr * 16), 0) * 4 + j
        xall[pl.ds(0, nvis), j * QUARTER : (j + 1) * QUARTER] = jnp.dot(
            jnp.where(gather, 1.0, 0.0).astype(BF16),
            arrived,
            preferred_element_type=F32,
        ).astype(BF16)
    x = xall[...]
    group = 8
    part[...] = jnp.zeros(part.shape, F32)

    @pl.loop(0, pool // group)
    def _(g):
        base = g * group
        block = lax.dot_general(
            pa[pl.ds(pl.multiple_of(base * rank, group * rank), group * rank), :],
            x,
            NT,
            preferred_element_type=F32,
        )
        picked = jnp.zeros((rank, ntot), F32)
        for s in range(group):
            picked += jnp.where(
                slot_row == base + s, block[s * rank : (s + 1) * rank], 0.0
            )
        part[:, :, pl.ds(0, ntot)] += picked.reshape(nt, kpart, ntot)

    @pl.loop(1, nt)
    def _(k):
        to = lax.rem(t + k, nt)
        pltpu.make_async_remote_copy(
            src_ref=part.at[to],
            dst_ref=rs_got.at[t],
            send_sem=rs_send,
            recv_sem=rs_recv,
            device_id=(r, to),
            device_id_type=MESH,
        ).start()

    ring_stage(2)
    cached_scores(rows // 2, rows)

    wait_bytes(stats.at[pl.ds(0, nt - 1)], st_recv)
    square = stats[0, 8:16, :]
    for k in range(1, nt):
        square += stats[k, 8:16, :]
    inverse_row = lax.rsqrt(square[0:1] / (width * nt) + EPS)
    inverse = jnp.sum(jnp.where(eye, inverse_row, 0.0), axis=1, keepdims=True)

    def project(o):
        source = lax.rem(t + o, nt)
        block = f_ref[...] if o == 0 else ring[o]
        block = block.astype(F32) * inverse
        gains = stats[source][0:8]
        normed = jnp.concatenate(
            [
                block[:, c * lanes : (c + 1) * lanes] * gains[c : c + 1]
                for c in range(chunks)
            ],
            axis=1,
        ).astype(BF16)
        w = wbuf[pl.ds(pl.multiple_of(source * width, width), width), :]
        product = jnp.dot(normed, w, preferred_element_type=F32)
        if o == 0:
            acc_kv[...] = product
        else:
            acc_kv[...] += product

    loads[2].wait()
    loads[3].wait()
    project(0)
    for h in range(1, half):
        if h >= 3:
            ring_stage(h)
        project(nt - h)
        project(h)

    wait_bytes(rs_got.at[pl.ds(0, nt - 1)], rs_recv)
    whole = part[t]
    for k in range(nt):
        whole += jnp.where(k == t, 0.0, rs_got[k])
    coeff[t] = whole

    @pl.loop(1, nt)
    def _(k):
        pltpu.make_async_remote_copy(
            src_ref=coeff.at[t],
            dst_ref=coeff.at[t],
            send_sem=ag_send,
            recv_sem=ag_recv,
            device_id=(r, lax.rem(t + k, nt)),
            device_id_type=MESH,
        ).start()

    loads[4].wait()
    pbt[...] = pb[...].T

    if half == 2:
        ring_stage(2)
    elif half >= 4:
        ring_stage(half)
    project(half)

    length_row = len_ref[...].astype(F32)
    positions = jnp.sum(
        jnp.where(eye_r, length_row, 0.0), axis=1, keepdims=True
    )
    positions = jnp.concatenate([positions, positions + 1.0], axis=0)
    angle = positions * freq_ref[...]
    sign = jnp.where(iota((rows2, HD), 1) < HD // 2, -1.0, 1.0)
    key = acc_kv[:, 0:HD]
    turned = key * jnp.cos(angle) + pltpu.roll(key, HD // 2, 1) * jnp.sin(angle) * sign
    new_keys = turned.astype(BF16)
    nk_ref[...] = new_keys

    qrows = 8
    span = qrows * per_row
    for b in range(rows // qrows):
        s = scores[b * qrows : (b + 1) * qrows].reshape(span, cache_len)
        q = q_ref[b * qrows : (b + 1) * qrows].reshape(span, HD)
        fresh = (
            lax.dot_general(q, new_keys, NT, preferred_element_type=F32) * scale
        )
        row_of = iota(fresh.shape, 0) // per_row + b * qrows
        step_of = iota(fresh.shape, 0) % per_row // GROUP
        column = iota(fresh.shape, 1)
        seen = (column == row_of) | ((column == row_of + rows) & (step_of == 1))
        fresh = jnp.where(seen, fresh, NEG)
        top = jnp.maximum(
            jnp.max(s, axis=1, keepdims=True), jnp.max(fresh, axis=1, keepdims=True)
        )
        e_cache = jnp.exp(s - top)
        e_fresh = jnp.exp(fresh - top)
        bottom = jnp.sum(e_cache, axis=1, keepdims=True) + jnp.sum(
            e_fresh, axis=1, keepdims=True
        )
        weights[b * qrows : (b + 1) * qrows] = (
            (e_cache / bottom).astype(BF16).reshape(qrows, per_row, cache_len)
        )
        fresh_w[b * span : (b + 1) * span, :] = (e_fresh / bottom).astype(BF16)

    wait_bytes(coeff.at[pl.ds(0, nt - 1)], ag_recv)
    coeffs = coeff[...].reshape(rank, coeff.shape[2])[:, 0:ntot]
    for s in range(pool):
        expand[s * rank : (s + 1) * rank, :] = jnp.where(
            slot_row == s, coeffs, 0.0
        ).astype(BF16)
    delta = jnp.dot(pbt[...], expand[...], preferred_element_type=F32).T
    ret_send[...] = delta[0:nvis]
    own_delta = delta[nvis:ntot]

    @pl.loop(1, nr)
    def _(k):
        to = lax.rem(r + k, nr)
        pltpu.make_async_remote_copy(
            src_ref=ret_send.at[pl.ds(pl.multiple_of(to // 2 * 8, 8), 8), :],
            dst_ref=ret_got.at[pl.ds(pl.multiple_of(r * 8, 8), 8), :],
            send_sem=re_send,
            recv_sem=re_recv,
            device_id=(to, t),
            device_id_type=MESH,
        ).start()

    loads[5].wait()

    @pl.loop(0, rows, unroll=4)
    def _(i):
        att_acc[i] = jnp.dot(weights[i], cv[i], preferred_element_type=F32)

    code_f = jnp.where(
        is_far, owner * 8 + lax.rem(r, 2) * 4 + turn * 2, -1000
    ).astype(F32)
    code_col = jnp.sum(jnp.where(eye_r, code_f, 0.0), axis=1, keepdims=True)
    code_col = jnp.concatenate([code_col, code_col + 1.0], axis=0).astype(jnp.int32)
    back = jnp.where(iota((rows2, nr * 8), 1) == code_col, 1.0, 0.0).astype(BF16)
    wait_bytes(ret_got.at[pl.ds(0, (nr - 1) * 8), :], re_recv)
    returned = ret_got[...]
    high = returned.astype(BF16)
    low = (returned - high.astype(F32)).astype(BF16)
    far_delta = jnp.dot(back, high, preferred_element_type=F32) + jnp.dot(
        back, low, preferred_element_type=F32
    )
    new_values = (acc_kv[:, HD : 2 * HD] + inverse * (far_delta + own_delta)).astype(
        BF16
    )
    nv_ref[...] = new_values
    mixed = att_acc[...].reshape(rows * per_row, HD) + jnp.dot(
        fresh_w[...], new_values, preferred_element_type=F32
    )
    att_ref[...] = mixed.astype(BF16).reshape(rows, per_row, HD)

    for h in range(1, half + 1):
        for way, c in hops(h):
            hop(way, h, c).wait_send()
    wait_bytes(stats.at[pl.ds(0, nt - 1)], st_send)
    wait_bytes(msg.at[pl.ds(0, (nr - 1) * 16), :], a2a_send)
    wait_bytes(part.at[pl.ds(0, nt - 1)], rs_send)
    wait_bytes(coeff.at[pl.ds(0, nt - 1)], ag_send)
    wait_bytes(ret_got.at[pl.ds(0, (nr - 1) * 8), :], re_send)


def shards(
    features,
    gain,
    w_key,
    w_value,
    pool_a,
    pool_b,
    placement,
    need_lists,
    row_adapter,
    lengths,
    queries,
    cache_k,
    cache_v,
):
    nr, nt = lax.axis_size("replica"), lax.axis_size("tp")
    steps, rows, width = features.shape
    pool, _, rank = pool_a.shape
    cache_len = cache_k.shape[1]
    rows2 = steps * rows
    nvis = nr * 4
    ntot = nvis + rows2
    ntot_pad = -(-ntot // HD) * HD
    per_row = steps * GROUP
    q = queries.reshape(steps, rows, GROUP, HD).transpose(1, 0, 2, 3)
    q = q.reshape(rows, per_row, HD)
    half = HD // 2
    frequency = np.float32(THETA) ** (-(np.arange(half, dtype=np.float32) * 2.0) / HD)
    frequency = np.concatenate([frequency, frequency]).astype(np.float32)[None, :]
    vmem = pl.BlockSpec(memory_space=pltpu.VMEM)
    smem = pl.BlockSpec(memory_space=pltpu.SMEM)
    hbm = pl.BlockSpec(memory_space=pl.ANY)
    dma = pltpu.SemaphoreType.DMA
    att, nk, nv = pl.pallas_call(
        functools.partial(kernel, nr, nt),
        out_shape=(
            jax.ShapeDtypeStruct((rows, per_row, HD), BF16),
            jax.ShapeDtypeStruct((rows2, HD), BF16),
            jax.ShapeDtypeStruct((rows2, HD), BF16),
        ),
        in_specs=[vmem] * 5 + [smem] + [vmem] * 3 + [hbm] * 6,
        out_specs=(vmem, vmem, vmem),
        scratch_shapes=[
            pltpu.VMEM((nt * width, 2 * HD), BF16),
            pltpu.VMEM((pool * rank, width), BF16),
            pltpu.VMEM((pool * rank, HD), BF16),
            pltpu.VMEM((HD, pool * rank), BF16),
            pltpu.VMEM((rows, cache_len, HD), BF16),
            pltpu.VMEM((rows, cache_len, HD), BF16),
            pltpu.VMEM((nt, 16, HD), F32),
            pltpu.VMEM((nr * 16, QUARTER), BF16),
            pltpu.VMEM((nr * 16, QUARTER), BF16),
            pltpu.VMEM((ntot, width), BF16),
            pltpu.VMEM((nt, rows2, width), BF16),
            pltpu.VMEM((nt, rank // nt, ntot_pad), F32),
            pltpu.VMEM((nt, rank // nt, ntot_pad), F32),
            pltpu.VMEM((nt, rank // nt, ntot_pad), F32),
            pltpu.VMEM((pool * rank, ntot), BF16),
            pltpu.VMEM((nvis, HD), F32),
            pltpu.VMEM((nr * 8, HD), F32),
            pltpu.VMEM((rows, per_row, cache_len), F32),
            pltpu.VMEM((rows, per_row, cache_len), BF16),
            pltpu.VMEM((rows * per_row, rows2), BF16),
            pltpu.VMEM((rows2, 2 * HD), F32),
            pltpu.VMEM((rows, per_row, HD), F32),
            dma((6,)),
            dma,
            dma,
            dma,
            dma,
            dma((2, max(nt // 2, 1), 2)),
            dma((nt, 2)),
            dma,
            dma,
            dma,
            dma,
            dma,
            dma,
        ],
        compiler_params=pltpu.CompilerParams(
            collective_id=0, has_side_effects=True, vmem_limit_bytes=48 * 2**20
        ),
        cost_estimate=pl.CostEstimate(
            flops=2 * 64 * 8192 * 256, bytes_accessed=12 * 2**20, transcendentals=0
        ),
    )(
        features.reshape(rows2, width),
        gain.reshape(1, width),
        placement.reshape(1, -1),
        need_lists.T,
        row_adapter.reshape(1, rows),
        lengths,
        lengths.reshape(1, rows),
        jnp.asarray(frequency),
        q,
        w_key,
        w_value,
        pool_a.swapaxes(1, 2).reshape(pool * rank, width),
        pool_b.reshape(pool * rank, HD),
        cache_k,
        cache_v,
    )
    attention = att.reshape(rows, steps, GROUP * HD).transpose(1, 0, 2)
    return attention, nk.reshape(steps, rows, HD), nv.reshape(steps, rows, HD)


def solution(mesh):
    placed = (
        P(None, "replica", "tp"),
        P("tp"),
        P(None, "tp"),
        P(None, "tp"),
        P("replica", "tp", None),
        P("replica", None, "tp"),
        P(),
        P(),
        P("replica"),
        P("replica"),
        P(None, "replica", "tp"),
        P("replica", None, "tp"),
        P("replica", None, "tp"),
    )
    return jax.shard_map(
        shards,
        mesh=mesh,
        in_specs=placed,
        out_specs=(P(None, "replica", "tp"), P(None, "replica", "tp"), P(None, "replica", "tp")),
        check_vma=False,
    )
```

time: 181 us -> 52.7 us (0.29)
  the two profiles are of different devices: /device:TPU:0 before, /device:TPU:1 now
where the time goes in v1:
time: 52.7 us; the launch traced here: 52.4 us
  Pallas kernels  38.4 us (73%)
  local copies, waits for them, and re-layouts  13.3 us (25%)
  between operations  0.67 us (1%)
    pallas_call x1, Pallas kernels, shards(): pl.pallas_call(functools.partial(kernel, nr, nt), out_shape=(jax.ShapeDty...  38.4 us
    unnamed x23, local copies, waits for them, and re-layouts  11.8 us

profile of v1, /device:TPU:1, one launch (start us, length us, event | category | flops | bytes accessed | tf_op | source)
XLA Modules:
  0.0 52.4 jit_solution(2840089013492388994)
XLA Ops:
  0.6 0.7 %reshape.43.gain_ref = bf16[1,1024]{1,0:T(2,128)(2,1)S(1)} reshape(bf16[1024]{0:T(1024)(128)(2,1)} %param.15) | data formatting | bytes 4096 | tf_op jit(solution)/shard_map/reshape | solution.py:566
  1.3 0.9 %copy.19 = bf16[8,8,8,128]{3,2,1,0:T(8,128)(2,1)S(1)} copy(bf16[8,8,8,128]{3,1,2,0:T(8,128)(2,1)} %bitcast.36) | data formatting | bytes 262144
  2.3 0.0 copy-start
  2.3 1.6 %copy-done = bf16[8192,128]{1,0:T(8,128)(2,1)S(1)} copy-done((bf16[8192,128]{1,0:T(8,128)(2,1)S(1)}, bf16[8192,128]{1,0:T(8,128)(2,1)}, u32[]{:S(2)}) %copy-start) | copy-done | bytes 2097176
  3.9 0.0 copy-start.1
  3.9 1.4 %copy-done.1 = bf16[32,192,128]{2,1,0:T(8,128)(2,1)S(1)} copy-done((bf16[32,192,128]{2,1,0:T(8,128)(2,1)S(1)}, bf16[32,192,128]{2,1,0:T(8,128)(2,1)}, u32[]{:S(2)}) %copy-start.1) | copy-done | bytes 1572888
  5.3 0.0 copy-start.2
  5.3 1.4 %copy-done.2 = bf16[32,192,128]{2,1,0:T(8,128)(2,1)S(1)} copy-done((bf16[32,192,128]{2,1,0:T(8,128)(2,1)S(1)}, bf16[32,192,128]{2,1,0:T(8,128)(2,1)}, u32[]{:S(2)}) %copy-start.2) | copy-done | bytes 1572888
  6.7 0.0 copy-start.3
  6.7 1.0 %copy-done.3 = bf16[32,64,128]{2,1,0:T(8,128)(2,1)S(1)} copy-done((bf16[32,64,128]{2,1,0:T(8,128)(2,1)S(1)}, bf16[32,64,128]{2,1,0:T(8,128)(2,1)}, u32[]{:S(2)}) %copy-start.3) | copy-done | bytes 524312
  7.7 0.0 copy-start.4
  7.7 0.9 %copy-done.4 = bf16[2,32,1024]{2,1,0:T(8,128)(2,1)S(1)} copy-done((bf16[2,32,1024]{2,1,0:T(8,128)(2,1)S(1)}, bf16[2,32,1024]{2,1,0:T(8,128)(2,1)}, u32[]{:S(2)}) %copy-start.4) | copy-done | bytes 131096
  8.6 0.0 copy-start.5
  8.6 0.7 %copy-done.5 = s32[32,16]{0,1:T(8,128)S(1)} copy-done((s32[32,16]{0,1:T(8,128)S(1)}, s32[32,16]{0,1:T(8,128)}, u32[]{:S(2)}) %copy-start.5) | copy-done | bytes 2072
  9.3 0.0 copy-start.6
  9.3 0.7 %copy-done.6 = s32[1024]{0:T(1024)S(1)} copy-done((s32[1024]{0:T(1024)S(1)}, s32[1024]{0:T(1024)}, u32[]{:S(2)}) %copy-start.6) | copy-done | bytes 4120
  10.0 0.0 copy-start.7
  10.0 0.7 %copy-done.7 = s32[32]{0:T(128)S(1)} copy-done((s32[32]{0:T(128)S(1)}, s32[32]{0:T(128)}, u32[]{:S(2)}) %copy-start.7) | copy-done | bytes 152
  10.7 0.0 copy-start.8
  10.7 0.7 %copy-done.8 = s32[32]{0:T(128)S(1)} copy-done((s32[32]{0:T(128)S(1)}, s32[32]{0:T(128)}, u32[]{:S(2)}) %copy-start.8) | copy-done | bytes 152
  11.3 0.0 copy-start.9
  11.3 0.7 %copy-done.9 = f32[1,128]{1,0:T(1,128)S(1)} copy-done((f32[1,128]{1,0:T(1,128)S(1)}, f32[1,128]{1,0:T(1,128)}, u32[]{:S(2)}) %copy-start.9) | copy-done | bytes 536
  12.0 38.4 %shard_map.157 = (bf16[32,16,128]{2,1,0:T(8,128)(2,1)S(1)}, bf16[64,128]{1,0:T(8,128)(2,1)S(1)}, bf16[64,128]{1,0:T(8,128)(2,1)S(1)}) custom-call(bf16[64,1024]{1,0:T(8,128)(2,1)S(1)} %bitcast.27, bf16[1,1024]{1,0:T(2,128)(2,1)S(1)} %reshape.43.gain_ref, s32[1,1024]{1,0:T(1,128)S(1)} %bitcast.31, s32[16,32]{1,0:T(8,128)S(1)} %bitcast.30, ...), custom_call_target="tpu_custom_call" | custom-call | flops 268435456 | bytes 12582912 | tf_op jit(solution)/shard_map/pallas_call | solution.py:512
  50.5 0.7 %copy.22 = bf16[32,2,1024]{2,0,1:T(8,128)(2,1)} copy(bf16[32,2,1024]{2,1,0:T(2,128)(2,1)S(1)} %reshape.51) | data formatting | bytes 262144 | tf_op jit(solution)/shard_map/reshape | solution.py:581
  51.2 0.6 %copy.25 = bf16[2,32,128]{2,1,0:T(8,128)(2,1)} copy(bf16[2,32,128]{2,1,0:T(8,128)(2,1)S(1)} %bitcast.29) | data formatting | bytes 32768
  51.8 0.6 %copy.26 = bf16[2,32,128]{2,1,0:T(8,128)(2,1)} copy(bf16[2,32,128]{2,1,0:T(8,128)(2,1)S(1)} %bitcast.28) | data formatting | bytes 32768
  (2 shorter events, 0.1 us)
Async XLA Ops:
  2.3 1.6 %copy-start = (bf16[8192,128]{1,0:T(8,128)(2,1)S(1)}, bf16[8192,128]{1,0:T(8,128)(2,1)}, u32[]{:S(2)}) copy-start(bf16[8192,128]{1,0:T(8,128)(2,1)} %wk_hbm.1) | copy-start | bytes 6291460
  3.9 1.4 %copy-start.1 = (bf16[32,192,128]{2,1,0:T(8,128)(2,1)S(1)}, bf16[32,192,128]{2,1,0:T(8,128)(2,1)}, u32[]{:S(2)}) copy-start(bf16[32,192,128]{2,1,0:T(8,128)(2,1)} %ck_hbm.1) | copy-start | bytes 4718596
  5.3 1.4 %copy-start.2 = (bf16[32,192,128]{2,1,0:T(8,128)(2,1)S(1)}, bf16[32,192,128]{2,1,0:T(8,128)(2,1)}, u32[]{:S(2)}) copy-start(bf16[32,192,128]{2,1,0:T(8,128)(2,1)} %cv_hbm.1) | copy-start | bytes 4718596
  6.7 1.0 %copy-start.3 = (bf16[32,64,128]{2,1,0:T(8,128)(2,1)S(1)}, bf16[32,64,128]{2,1,0:T(8,128)(2,1)}, u32[]{:S(2)}) copy-start(bf16[32,64,128]{2,1,0:T(8,128)(2,1)} %param.19) | copy-start | bytes 1572868
  7.7 0.9 %copy-start.4 = (bf16[2,32,1024]{2,1,0:T(8,128)(2,1)S(1)}, bf16[2,32,1024]{2,1,0:T(8,128)(2,1)}, u32[]{:S(2)}) copy-start(bf16[2,32,1024]{2,1,0:T(8,128)(2,1)} %param.14) | copy-start | bytes 393220
  8.6 0.7 %copy-start.5 = (s32[32,16]{0,1:T(8,128)S(1)}, s32[32,16]{0,1:T(8,128)}, u32[]{:S(2)}) copy-start(s32[32,16]{0,1:T(8,128)} %param.21) | copy-start | bytes 6148
  9.3 0.7 %copy-start.6 = (s32[1024]{0:T(1024)S(1)}, s32[1024]{0:T(1024)}, u32[]{:S(2)}) copy-start(s32[1024]{0:T(1024)} %param.20) | copy-start | bytes 12292
  10.0 0.7 %copy-start.7 = (s32[32]{0:T(128)S(1)}, s32[32]{0:T(128)}, u32[]{:S(2)}) copy-start(s32[32]{0:T(128)} %len_s.1) | copy-start | bytes 388
  10.7 0.7 %copy-start.8 = (s32[32]{0:T(128)S(1)}, s32[32]{0:T(128)}, u32[]{:S(2)}) copy-start(s32[32]{0:T(128)} %param.22) | copy-start | bytes 388
  11.3 0.7 %copy-start.9 = (f32[1,128]{1,0:T(1,128)S(1)}, f32[1,128]{1,0:T(1,128)}, u32[]{:S(2)}) copy-start(f32[1,128]{1,0:T(1,128)} %constant.2.clone.freq_ref) | copy-start | bytes 1540

commit v2 on v1

--- a/solution.py
+++ b/solution.py
@@ -28,15 +28,15 @@
 def kernel(
     nr,
     nt,
-    f_ref,
-    gain_ref,
-    place_ref,
-    need_ref,
-    ra_ref,
-    len_s,
-    len_ref,
-    freq_ref,
-    q_ref,
+    f_hbm,
+    gain_hbm,
+    place_hbm,
+    need_hbm,
+    ra_hbm,
+    len_s_hbm,
+    len_hbm,
+    freq_hbm,
+    q_hbm,
     wk_hbm,
     wv_hbm,
     pa_hbm,
@@ -46,6 +46,17 @@
     att_ref,
     nk_ref,
     nv_ref,
+    f_ref,
+    gain_ref,
+    place_ref,
+    need_ref,
+    ra_ref,
+    len_s,
+    len_ref,
+    freq_ref,
+    q_in,
+    q_wide,
+    q_ref,
     wbuf,
     pa,
     pb,
@@ -68,6 +79,7 @@
     fresh_w,
     acc_kv,
     att_acc,
+    small_sem,
     load_sem,
     st_send,
     st_recv,
@@ -94,6 +106,22 @@
     nvis = nr * 4
     ntot = nvis + rows2
 
+    small = [
+        pltpu.make_async_copy(a, b, small_sem.at[k])
+        for k, (a, b) in enumerate(
+            [
+                (f_hbm, f_ref),
+                (gain_hbm, gain_ref),
+                (ra_hbm, ra_ref),
+                (need_hbm, need_ref),
+                (place_hbm, place_ref),
+                (len_s_hbm, len_s),
+                (len_hbm, len_ref),
+                (freq_hbm, freq_ref),
+                (q_hbm, q_in),
+            ]
+        )
+    ]
     loads = [
         pltpu.make_async_copy(ck_hbm, ck, load_sem.at[0]),
         pltpu.make_async_copy(pa_hbm, pa, load_sem.at[1]),
@@ -102,7 +130,7 @@
         pltpu.make_async_copy(pb_hbm, pb, load_sem.at[4]),
         pltpu.make_async_copy(cv_hbm, cv, load_sem.at[5]),
     ]
-    for load in loads:
+    for load in small + loads:
         load.start()
 
     barrier = pltpu.get_barrier_semaphore()
@@ -119,22 +147,29 @@
             barrier, inc=1, device_id=(r, lax.rem(t + k, nt)), device_id_type=MESH
         )
 
-    gain = gain_ref[...].astype(F32)
+    small[0].wait()
+    small[1].wait()
+    gain_rows = gain_ref[...].astype(F32)
     f32 = f_ref[...].astype(F32)
     lanes = HD
     chunks = width // lanes
     eye = iota((rows2, lanes), 0) == iota((rows2, lanes), 1)
     square_sum = jnp.sum(f32 * f32, axis=1, keepdims=True)
     square_row = jnp.sum(jnp.where(eye, square_sum, 0.0), axis=0, keepdims=True)
-    gain_rows = jnp.concatenate(
-        [gain[:, c * lanes : (c + 1) * lanes] for c in range(chunks)], axis=0
-    )
     stats[t] = jnp.concatenate(
         [gain_rows, jnp.broadcast_to(square_row, (8, lanes))], axis=0
     )
-    own = (f32 * gain).astype(BF16)
+    own = jnp.concatenate(
+        [
+            f32[:, c * lanes : (c + 1) * lanes] * gain_rows[c : c + 1]
+            for c in range(chunks)
+        ],
+        axis=1,
+    ).astype(BF16)
     xall[pl.ds(nvis, rows2), :] = own
 
+    for load in small[2:5]:
+        load.wait()
     ra = ra_ref[...]
     need = need_ref[...]
     mine = jnp.sum(
@@ -262,15 +297,27 @@
             live = iota(s.shape, 1) < len_s[i]
             scores[i] = jnp.where(live, s, NEG)
 
-    def ring_stage(h):
+    def ring_stage(h, which_chunks=(0, 1)):
         for way, c in hops(h):
+            if c not in which_chunks:
+                continue
             hop(way, h, c).wait_recv()
             if (way, c) in (hops(h + 1) if h < half else []):
                 hop(way, h + 1, c).start()
 
+    for load in small[5:]:
+        load.wait()
+    for step in range(2):
+        for g in range(GROUP):
+            q_wide[pl.ds(step * GROUP + g, rows, stride=per_row), :] = q_in[
+                step * rows : (step + 1) * rows, g * HD : (g + 1) * HD
+            ].astype(F32)
+    q_ref[...] = q_wide[...].astype(BF16).reshape(rows, per_row, HD)
     loads[0].wait()
-    cached_scores(0, rows // 2)
-    ring_stage(1)
+    cached_scores(0, rows // 4)
+    ring_stage(1, (0,))
+    cached_scores(rows // 4, rows // 2)
+    ring_stage(1, (1,))
 
     loads[1].wait()
     wait_bytes(got.at[pl.ds(0, (nr - 1) * 16), :], a2a_recv)
@@ -314,8 +361,8 @@
             device_id_type=MESH,
         ).start()
 
-    ring_stage(2)
-    cached_scores(rows // 2, rows)
+    if half > 2:
+        ring_stage(2)
 
     wait_bytes(stats.at[pl.ds(0, nt - 1)], st_recv)
     square = stats[0, 8:16, :]
@@ -346,11 +393,9 @@
     loads[2].wait()
     loads[3].wait()
     project(0)
-    for h in range(1, half):
-        if h >= 3:
-            ring_stage(h)
-        project(nt - h)
-        project(h)
+    project(nt - 1)
+    if half > 1:
+        project(1)
 
     wait_bytes(rs_got.at[pl.ds(0, nt - 1)], rs_recv)
     whole = part[t]
@@ -369,52 +414,14 @@
             device_id_type=MESH,
         ).start()
 
+    for h in range(2, half):
+        if h > 2:
+            ring_stage(h)
+        project(nt - h)
+        project(h)
+    cached_scores(rows // 2, rows)
     loads[4].wait()
     pbt[...] = pb[...].T
-
-    if half == 2:
-        ring_stage(2)
-    elif half >= 4:
-        ring_stage(half)
-    project(half)
-
-    length_row = len_ref[...].astype(F32)
-    positions = jnp.sum(
-        jnp.where(eye_r, length_row, 0.0), axis=1, keepdims=True
-    )
-    positions = jnp.concatenate([positions, positions + 1.0], axis=0)
-    angle = positions * freq_ref[...]
-    sign = jnp.where(iota((rows2, HD), 1) < HD // 2, -1.0, 1.0)
-    key = acc_kv[:, 0:HD]
-    turned = key * jnp.cos(angle) + pltpu.roll(key, HD // 2, 1) * jnp.sin(angle) * sign
-    new_keys = turned.astype(BF16)
-    nk_ref[...] = new_keys
-
-    qrows = 8
-    span = qrows * per_row
-    for b in range(rows // qrows):
-        s = scores[b * qrows : (b + 1) * qrows].reshape(span, cache_len)
-        q = q_ref[b * qrows : (b + 1) * qrows].reshape(span, HD)
-        fresh = (
-            lax.dot_general(q, new_keys, NT, preferred_element_type=F32) * scale
-        )
-        row_of = iota(fresh.shape, 0) // per_row + b * qrows
-        step_of = iota(fresh.shape, 0) % per_row // GROUP
-        column = iota(fresh.shape, 1)
-        seen = (column == row_of) | ((column == row_of + rows) & (step_of == 1))
-        fresh = jnp.where(seen, fresh, NEG)
-        top = jnp.maximum(
-            jnp.max(s, axis=1, keepdims=True), jnp.max(fresh, axis=1, keepdims=True)
-        )
-        e_cache = jnp.exp(s - top)
-        e_fresh = jnp.exp(fresh - top)
-        bottom = jnp.sum(e_cache, axis=1, keepdims=True) + jnp.sum(
-            e_fresh, axis=1, keepdims=True
-        )
-        weights[b * qrows : (b + 1) * qrows] = (
-            (e_cache / bottom).astype(BF16).reshape(qrows, per_row, cache_len)
-        )
-        fresh_w[b * span : (b + 1) * span, :] = (e_fresh / bottom).astype(BF16)
 
     wait_bytes(coeff.at[pl.ds(0, nt - 1)], ag_recv)
     coeffs = coeff[...].reshape(rank, coeff.shape[2])[:, 0:ntot]
@@ -438,11 +445,52 @@
             device_id_type=MESH,
         ).start()
 
+    ring_stage(half)
+    project(half)
+
+    length_row = len_ref[...].astype(F32)
+    positions = jnp.sum(
+        jnp.where(eye_r, length_row, 0.0), axis=1, keepdims=True
+    )
+    positions = jnp.concatenate([positions, positions + 1.0], axis=0)
+    angle = positions * freq_ref[...]
+    sign = jnp.where(iota((rows2, HD), 1) < HD // 2, -1.0, 1.0)
+    key = acc_kv[:, 0:HD]
+    turned = key * jnp.cos(angle) + pltpu.roll(key, HD // 2, 1) * jnp.sin(angle) * sign
+    new_keys = turned.astype(BF16)
+    nk_ref[...] = new_keys
+
+    qrows = 8
+    span = qrows * per_row
+    for b in range(rows // qrows):
+        s = scores[b * qrows : (b + 1) * qrows].reshape(span, cache_len)
+        q = q_ref[b * qrows : (b + 1) * qrows].reshape(span, HD)
+        fresh = (
+            lax.dot_general(q, new_keys, NT, preferred_element_type=F32) * scale
+        )
+        row_of = iota(fresh.shape, 0) // per_row + b * qrows
+        step_of = iota(fresh.shape, 0) % per_row // GROUP
+        column = iota(fresh.shape, 1)
+        seen = (column == row_of) | ((column == row_of + rows) & (step_of == 1))
+        fresh = jnp.where(seen, fresh, NEG)
+        top = jnp.maximum(
+            jnp.max(s, axis=1, keepdims=True), jnp.max(fresh, axis=1, keepdims=True)
+        )
+        e_cache = jnp.exp(s - top)
+        e_fresh = jnp.exp(fresh - top)
+        bottom = jnp.sum(e_cache, axis=1, keepdims=True) + jnp.sum(
+            e_fresh, axis=1, keepdims=True
+        )
+        weights[b * qrows : (b + 1) * qrows] = (
+            (e_cache / bottom).astype(BF16).reshape(qrows, per_row, cache_len)
+        )
+        fresh_w[b * span : (b + 1) * span, :] = (e_fresh / bottom).astype(BF16)
+
     loads[5].wait()
 
     @pl.loop(0, rows, unroll=4)
     def _(i):
-        att_acc[i] = jnp.dot(weights[i], cv[i], preferred_element_type=F32)
+        att_acc[pl.ds(pl.multiple_of(i * per_row, per_row), per_row), :] = jnp.dot(weights[i], cv[i], preferred_element_type=F32)
 
     code_f = jnp.where(
         is_far, owner * 8 + lax.rem(r, 2) * 4 + turn * 2, -1000
@@ -461,10 +509,12 @@
         BF16
     )
     nv_ref[...] = new_values
-    mixed = att_acc[...].reshape(rows * per_row, HD) + jnp.dot(
-        fresh_w[...], new_values, preferred_element_type=F32
-    )
-    att_ref[...] = mixed.astype(BF16).reshape(rows, per_row, HD)
+    att_acc[...] += jnp.dot(fresh_w[...], new_values, preferred_element_type=F32)
+    for step in range(2):
+        for g in range(GROUP):
+            att_ref[step * rows : (step + 1) * rows, g * HD : (g + 1) * HD] = att_acc[
+                pl.ds(step * GROUP + g, rows, stride=per_row), :
+            ].astype(BF16)
 
     for h in range(1, half + 1):
         for way, c in hops(h):
@@ -474,6 +524,17 @@
     wait_bytes(part.at[pl.ds(0, nt - 1)], rs_send)
     wait_bytes(coeff.at[pl.ds(0, nt - 1)], ag_send)
     wait_bytes(ret_got.at[pl.ds(0, (nr - 1) * 8), :], re_send)
+
+
+def write_out(a, b, c, a_out, b_out, c_out, sem):
+    copies = [
+        pltpu.make_async_copy(src, dst, sem.at[k])
+        for k, (src, dst) in enumerate([(a, a_out), (b, b_out), (c, c_out)])
+    ]
+    for copy in copies:
+        copy.start()
+    for copy in copies:
+        copy.wait()
 
 
 def shards(
@@ -500,25 +561,33 @@
     ntot = nvis + rows2
     ntot_pad = -(-ntot // HD) * HD
     per_row = steps * GROUP
-    q = queries.reshape(steps, rows, GROUP, HD).transpose(1, 0, 2, 3)
-    q = q.reshape(rows, per_row, HD)
     half = HD // 2
     frequency = np.float32(THETA) ** (-(np.arange(half, dtype=np.float32) * 2.0) / HD)
     frequency = np.concatenate([frequency, frequency]).astype(np.float32)[None, :]
     vmem = pl.BlockSpec(memory_space=pltpu.VMEM)
-    smem = pl.BlockSpec(memory_space=pltpu.SMEM)
-    hbm = pl.BlockSpec(memory_space=pl.ANY)
+    hbm = pl.BlockSpec(memory_space=pltpu.HBM)
     dma = pltpu.SemaphoreType.DMA
     att, nk, nv = pl.pallas_call(
         functools.partial(kernel, nr, nt),
         out_shape=(
-            jax.ShapeDtypeStruct((rows, per_row, HD), BF16),
+            jax.ShapeDtypeStruct((rows2, width), BF16),
             jax.ShapeDtypeStruct((rows2, HD), BF16),
             jax.ShapeDtypeStruct((rows2, HD), BF16),
         ),
-        in_specs=[vmem] * 5 + [smem] + [vmem] * 3 + [hbm] * 6,
+        in_specs=[hbm] * 15,
         out_specs=(vmem, vmem, vmem),
         scratch_shapes=[
+            pltpu.VMEM((rows2, width), BF16),
+            pltpu.VMEM((width // HD, HD), BF16),
+            pltpu.VMEM((1, placement.shape[0]), jnp.int32),
+            pltpu.VMEM(need_lists.shape[::-1], jnp.int32),
+            pltpu.VMEM((1, rows), jnp.int32),
+            pltpu.SMEM((rows,), jnp.int32),
+            pltpu.VMEM((1, rows), jnp.int32),
+            pltpu.VMEM((1, HD), F32),
+            pltpu.VMEM((rows2, width), BF16),
+            pltpu.VMEM((rows * per_row, HD), F32),
+            pltpu.VMEM((rows, per_row, HD), BF16),
             pltpu.VMEM((nt * width, 2 * HD), BF16),
             pltpu.VMEM((pool * rank, width), BF16),
             pltpu.VMEM((pool * rank, HD), BF16),
@@ -540,7 +609,8 @@
             pltpu.VMEM((rows, per_row, cache_len), BF16),
             pltpu.VMEM((rows * per_row, rows2), BF16),
             pltpu.VMEM((rows2, 2 * HD), F32),
-            pltpu.VMEM((rows, per_row, HD), F32),
+            pltpu.VMEM((rows * per_row, HD), F32),
+            dma((9,)),
             dma((6,)),
             dma,
             dma,
@@ -556,21 +626,21 @@
             dma,
         ],
         compiler_params=pltpu.CompilerParams(
-            collective_id=0, has_side_effects=True, vmem_limit_bytes=48 * 2**20
+            collective_id=0, has_side_effects=True, vmem_limit_bytes=60 * 2**20
         ),
         cost_estimate=pl.CostEstimate(
             flops=2 * 64 * 8192 * 256, bytes_accessed=12 * 2**20, transcendentals=0
         ),
     )(
         features.reshape(rows2, width),
-        gain.reshape(1, width),
+        gain.reshape(width // HD, HD),
         placement.reshape(1, -1),
         need_lists.T,
         row_adapter.reshape(1, rows),
         lengths,
         lengths.reshape(1, rows),
         jnp.asarray(frequency),
-        q,
+        queries.reshape(rows2, width),
         w_key,
         w_value,
         pool_a.swapaxes(1, 2).reshape(pool * rank, width),
@@ -578,8 +648,19 @@
         cache_k,
         cache_v,
     )
-    attention = att.reshape(rows, steps, GROUP * HD).transpose(1, 0, 2)
-    return attention, nk.reshape(steps, rows, HD), nv.reshape(steps, rows, HD)
+    shapes = tuple(jax.ShapeDtypeStruct(x.shape, BF16) for x in (att, nk, nv))
+    att, nk, nv = pl.pallas_call(
+        write_out,
+        out_shape=shapes,
+        in_specs=[hbm] * 3,
+        out_specs=(hbm,) * 3,
+        scratch_shapes=[dma((3,))],
+    )(att, nk, nv)
+    return (
+        att.reshape(steps, rows, width),
+        nk.reshape(steps, rows, HD),
+        nv.reshape(steps, rows, HD),
+    )
 
 
 def solution(mesh):

time: 52.7 us -> 43.5 us (0.83)
  local copies, waits for them, and re-layouts: 13.3 us -> 0 us
  Pallas kernels: 38.4 us -> 42.8 us
    unnamed x23 -> x0, local copies, waits for them, and re-layouts: 11.8 us -> none
    pallas_call x0 -> x1, Pallas kernels: none -> 6.09 us  [shards(): pl.pallas_call(write_out, out_shape=shapes, in_specs=[hbm] * 3, out_specs...]
    pallas_call x1, Pallas kernels: 38.4 us -> 36.7 us  [shards(): pl.pallas_call(functools.partial(kernel, nr, nt), out_shape=(jax.ShapeDty...]
    reshape x4 -> x0, local copies, waits for them, and re-layouts: 1.43 us -> none  [the longest x2 0.72 us: shards(): attention = att.reshape(rows, steps, GROUP * HD).transpose(1, 0, 2)]
where the time goes in v2:
time: 43.5 us; the launch traced here: 43.4 us
  Pallas kernels  42.8 us (98%)
  between operations  0.64 us (1%)
    pallas_call x1, Pallas kernels, shards(): pl.pallas_call(functools.partial(kernel, nr, nt), out_shape=(jax.ShapeDty...  36.7 us
    pallas_call x1, Pallas kernels, shards(): pl.pallas_call(write_out, out_shape=shapes, in_specs=[hbm] * 3, out_specs...  6.09 us

profile of v2, /device:TPU:1, one launch (start us, length us, event | category | flops | bytes accessed | tf_op | source)
XLA Modules:
  0.0 43.4 jit_solution(12449581434857556941)
XLA Ops:
  0.6 36.7 %shard_map.157 = (bf16[64,1024]{1,0:T(8,128)(2,1)}, bf16[64,128]{1,0:T(8,128)(2,1)}, bf16[64,128]{1,0:T(8,128)(2,1)}) custom-call(bf16[64,1024]{1,0:T(8,128)(2,1)} %bitcast.16, bf16[8,128]{1,0:T(8,128)(2,1)} %bitcast.20, s32[1,1024]{1,0:T(1,128)} %bitcast.19, s32[16,32]{1,0:T(8,128)} %bitcast.18, s32[1,32]{1,0:T(1,128)} %bitcast.22, s32[32]{0:T(128)} %len_s_hbm.1, ...), custom_call_target="tpu_custom_call" | custom-call | flops 268435456 | bytes 12582912 | tf_op jit(solution)/shard_map/pallas_call | solution.py:570
  37.3 6.1 %shard_map.158 = (bf16[64,1024]{1,0:T(8,128)(2,1)}, bf16[64,128]{1,0:T(8,128)(2,1)}, bf16[64,128]{1,0:T(8,128)(2,1)}) custom-call(bf16[64,1024]{1,0:T(8,128)(2,1)} %get-tuple-element.9.a, bf16[64,128]{1,0:T(8,128)(2,1)} %get-tuple-element.10.b, bf16[64,128]{1,0:T(8,128)(2,1)} %get-tuple-element.11.c), custom_call_target="tpu_custom_call" | custom-call | tf_op jit(solution)/shard_map/pallas_call | solution.py:652

commit v3 on v2

--- a/solution.py
+++ b/solution.py
@@ -79,6 +79,10 @@
     fresh_w,
     acc_kv,
     att_acc,
+    top_ref,
+    bottom_ref,
+    cos_ref,
+    sin_ref,
     small_sem,
     load_sem,
     st_send,
@@ -316,7 +320,7 @@
     loads[0].wait()
     cached_scores(0, rows // 4)
     ring_stage(1, (0,))
-    cached_scores(rows // 4, rows // 2)
+    cached_scores(rows // 4, rows)
     ring_stage(1, (1,))
 
     loads[1].wait()
@@ -363,6 +367,20 @@
 
     if half > 2:
         ring_stage(2)
+
+    qrows = 8
+    span = qrows * per_row
+    for b in range(rows // qrows):
+        s = scores[b * qrows : (b + 1) * qrows].reshape(span, cache_len)
+        top = jnp.max(s, axis=1, keepdims=True)
+        e_cache = jnp.exp(s - top)
+        top_ref[b * span : (b + 1) * span, :] = top
+        bottom_ref[b * span : (b + 1) * span, :] = jnp.sum(
+            e_cache, axis=1, keepdims=True
+        )
+        weights[b * qrows : (b + 1) * qrows] = e_cache.astype(BF16).reshape(
+            qrows, per_row, cache_len
+        )
 
     wait_bytes(stats.at[pl.ds(0, nt - 1)], st_recv)
     square = stats[0, 8:16, :]
@@ -397,6 +415,16 @@
     if half > 1:
         project(1)
 
+    length_row = len_ref[...].astype(F32)
+    positions = jnp.sum(
+        jnp.where(eye_r, length_row, 0.0), axis=1, keepdims=True
+    )
+    positions = jnp.concatenate([positions, positions + 1.0], axis=0)
+    angle = positions * freq_ref[...]
+    sign = jnp.where(iota((rows2, HD), 1) < HD // 2, -1.0, 1.0)
+    cos_ref[...] = jnp.cos(angle)
+    sin_ref[...] = jnp.sin(angle) * sign
+
     wait_bytes(rs_got.at[pl.ds(0, nt - 1)], rs_recv)
     whole = part[t]
     for k in range(nt):
@@ -414,12 +442,19 @@
             device_id_type=MESH,
         ).start()
 
-    for h in range(2, half):
-        if h > 2:
-            ring_stage(h)
-        project(nt - h)
-        project(h)
-    cached_scores(rows // 2, rows)
+    for h in range(3, half):
+        ring_stage(h)
+        project(nt - h + 1)
+        project(h - 1)
+
+    loads[5].wait()
+
+    @pl.loop(0, rows, unroll=4)
+    def _(i):
+        att_acc[pl.ds(pl.multiple_of(i * per_row, per_row), per_row), :] = jnp.dot(
+            weights[i], cv[i], preferred_element_type=F32
+        )
+
     loads[4].wait()
     pbt[...] = pb[...].T
 
@@ -445,25 +480,19 @@
             device_id_type=MESH,
         ).start()
 
+    if half > 2:
+        project(nt - half + 1)
+        project(half - 1)
     ring_stage(half)
     project(half)
 
-    length_row = len_ref[...].astype(F32)
-    positions = jnp.sum(
-        jnp.where(eye_r, length_row, 0.0), axis=1, keepdims=True
-    )
-    positions = jnp.concatenate([positions, positions + 1.0], axis=0)
-    angle = positions * freq_ref[...]
-    sign = jnp.where(iota((rows2, HD), 1) < HD // 2, -1.0, 1.0)
     key = acc_kv[:, 0:HD]
-    turned = key * jnp.cos(angle) + pltpu.roll(key, HD // 2, 1) * jnp.sin(angle) * sign
+    turned = key * cos_ref[...] + pltpu.roll(key, HD // 2, 1) * sin_ref[...]
     new_keys = turned.astype(BF16)
     nk_ref[...] = new_keys
 
-    qrows = 8
-    span = qrows * per_row
     for b in range(rows // qrows):
-        s = scores[b * qrows : (b + 1) * qrows].reshape(span, cache_len)
+        part_rows = slice(b * span, (b + 1) * span)
         q = q_ref[b * qrows : (b + 1) * qrows].reshape(span, HD)
         fresh = (
             lax.dot_general(q, new_keys, NT, preferred_element_type=F32) * scale
@@ -473,24 +502,16 @@
         column = iota(fresh.shape, 1)
         seen = (column == row_of) | ((column == row_of + rows) & (step_of == 1))
         fresh = jnp.where(seen, fresh, NEG)
-        top = jnp.maximum(
-            jnp.max(s, axis=1, keepdims=True), jnp.max(fresh, axis=1, keepdims=True)
-        )
-        e_cache = jnp.exp(s - top)
+        cache_top = top_ref[part_rows, :]
+        top = jnp.maximum(cache_top, jnp.max(fresh, axis=1, keepdims=True))
+        shrink = jnp.exp(cache_top - top)
         e_fresh = jnp.exp(fresh - top)
-        bottom = jnp.sum(e_cache, axis=1, keepdims=True) + jnp.sum(
+        bottom = bottom_ref[part_rows, :] * shrink + jnp.sum(
             e_fresh, axis=1, keepdims=True
         )
-        weights[b * qrows : (b + 1) * qrows] = (
-            (e_cache / bottom).astype(BF16).reshape(qrows, per_row, cache_len)
-        )
-        fresh_w[b * span : (b + 1) * span, :] = (e_fresh / bottom).astype(BF16)
-
-    loads[5].wait()
-
-    @pl.loop(0, rows, unroll=4)
-    def _(i):
-        att_acc[pl.ds(pl.multiple_of(i * per_row, per_row), per_row), :] = jnp.dot(weights[i], cv[i], preferred_element_type=F32)
+        share = 1.0 / bottom
+        fresh_w[part_rows, :] = (e_fresh * share).astype(BF16)
+        att_acc[part_rows, :] = att_acc[part_rows, :] * (shrink * share)
 
     code_f = jnp.where(
         is_far, owner * 8 + lax.rem(r, 2) * 4 + turn * 2, -1000
@@ -610,6 +631,10 @@
             pltpu.VMEM((rows * per_row, rows2), BF16),
             pltpu.VMEM((rows2, 2 * HD), F32),
             pltpu.VMEM((rows * per_row, HD), F32),
+            pltpu.VMEM((rows * per_row, 1), F32),
+            pltpu.VMEM((rows * per_row, 1), F32),
+            pltpu.VMEM((rows2, HD), F32),
+            pltpu.VMEM((rows2, HD), F32),
             dma((9,)),
             dma((6,)),
             dma,
@@ -652,9 +677,10 @@
     att, nk, nv = pl.pallas_call(
         write_out,
         out_shape=shapes,
-        in_specs=[hbm] * 3,
+        in_specs=[vmem] * 3,
         out_specs=(hbm,) * 3,
         scratch_shapes=[dma((3,))],
+        compiler_params=pltpu.CompilerParams(vmem_limit_bytes=60 * 2**20),
     )(att, nk, nv)
     return (
         att.reshape(steps, rows, width),

time: 43.5 us -> 39.1 us (0.90)
  Pallas kernels: 42.8 us -> 38.3 us
    pallas_call x1, Pallas kernels: 6.09 us -> 1.61 us  [shards(): pl.pallas_call(write_out, out_shape=shapes, in_specs=[vmem] * 3, out_spec...]
where the time goes in v3:
time: 39.1 us; the launch traced here: 39 us
  Pallas kernels  38.3 us (98%)
  between operations  0.64 us (2%)
    pallas_call x1, Pallas kernels, shards(): pl.pallas_call(functools.partial(kernel, nr, nt), out_shape=(jax.ShapeDty...  36.7 us
    pallas_call x1, Pallas kernels, shards(): pl.pallas_call(write_out, out_shape=shapes, in_specs=[vmem] * 3, out_spec...  1.61 us

profile of v3, /device:TPU:1, one launch (start us, length us, event | category | flops | bytes accessed | tf_op | source)
XLA Modules:
  0.0 39.0 jit_solution(13855795673804727110)
XLA Ops:
  0.6 36.7 %shard_map.157 = (bf16[64,1024]{1,0:T(8,128)(2,1)}, bf16[64,128]{1,0:T(8,128)(2,1)}, bf16[64,128]{1,0:T(8,128)(2,1)}) custom-call(bf16[64,1024]{1,0:T(8,128)(2,1)} %bitcast.16, bf16[8,128]{1,0:T(8,128)(2,1)} %bitcast.20, s32[1,1024]{1,0:T(1,128)} %bitcast.19, s32[16,32]{1,0:T(8,128)} %bitcast.18, s32[1,32]{1,0:T(1,128)} %bitcast.22, s32[32]{0:T(128)} %len_s_hbm.1, ...), custom_call_target="tpu_custom_call" | custom-call | flops 268435456 | bytes 12582912 | tf_op jit(solution)/shard_map/pallas_call | solution.py:591
  37.4 1.6 %shard_map.158 = (bf16[64,1024]{1,0:T(8,128)(2,1)}, bf16[64,128]{1,0:T(8,128)(2,1)}, bf16[64,128]{1,0:T(8,128)(2,1)}) custom-call(bf16[64,1024]{1,0:T(8,128)(2,1)} %get-tuple-element.9.a, bf16[64,128]{1,0:T(8,128)(2,1)} %get-tuple-element.10.b, bf16[64,128]{1,0:T(8,128)(2,1)} %get-tuple-element.11.c), custom_call_target="tpu_custom_call" | custom-call | tf_op jit(solution)/shard_map/pallas_call | solution.py:677

commit v4 on v3

--- a/solution.py
+++ b/solution.py
@@ -134,22 +134,52 @@
         pltpu.make_async_copy(pb_hbm, pb, load_sem.at[4]),
         pltpu.make_async_copy(cv_hbm, cv, load_sem.at[5]),
     ]
-    for load in small + loads:
-        load.start()
 
     barrier = pltpu.get_barrier_semaphore()
 
-    @pl.loop(1, nr)
+    @pl.loop(1, nr, unroll=True)
     def _(k):
         pl.semaphore_signal(
             barrier, inc=1, device_id=(lax.rem(r + k, nr), t), device_id_type=MESH
         )
 
-    @pl.loop(1, nt)
+    @pl.loop(1, nt, unroll=True)
     def _(k):
         pl.semaphore_signal(
             barrier, inc=1, device_id=(r, lax.rem(t + k, nt)), device_id_type=MESH
         )
+
+    for load in small + loads:
+        load.start()
+    pl.semaphore_wait(barrier, nr - 1 + nt - 1)
+
+    right = (r, lax.rem(t + 1, nt))
+    left = (r, lax.rem(t + nt - 1, nt))
+    half = nt // 2
+
+    def hop(which_way, h, c):
+        if which_way == 0:
+            have, there, to = (nt - (h - 1)) % nt, nt - h, right
+        else:
+            have, there, to = h - 1, h, left
+        piece = pl.ds(c * rows, rows)
+        src = f_hbm.at[piece, :] if have == 0 else ring.at[have, piece, :]
+        return pltpu.make_async_remote_copy(
+            src_ref=src,
+            dst_ref=ring.at[there, piece, :],
+            send_sem=ring_send.at[which_way, h - 1, c],
+            recv_sem=ring_recv.at[there, c],
+            device_id=to,
+            device_id_type=MESH,
+        )
+
+    def hops(h):
+        if h < half:
+            return [(0, 0), (1, 0), (0, 1), (1, 1)]
+        return [(0, 0), (1, 1)]
+
+    for way, c in hops(1):
+        hop(way, 1, c).start()
 
     small[0].wait()
     small[1].wait()
@@ -163,6 +193,17 @@
     stats[t] = jnp.concatenate(
         [gain_rows, jnp.broadcast_to(square_row, (8, lanes))], axis=0
     )
+    @pl.loop(1, nt, unroll=True)
+    def _(k):
+        pltpu.make_async_remote_copy(
+            src_ref=stats.at[t],
+            dst_ref=stats.at[t],
+            send_sem=st_send,
+            recv_sem=st_recv,
+            device_id=(r, lax.rem(t + k, nt)),
+            device_id_type=MESH,
+        ).start()
+
     own = jnp.concatenate(
         [
             f32[:, c * lanes : (c + 1) * lanes] * gain_rows[c : c + 1]
@@ -218,48 +259,7 @@
     got[pl.ds(pl.multiple_of(r * 16, 16), 16), :] = jnp.zeros((16, QUARTER), BF16)
     ret_got[pl.ds(pl.multiple_of(r * 8, 8), 8), :] = jnp.zeros((8, HD), F32)
 
-    pl.semaphore_wait(barrier, nr - 1 + nt - 1)
-
-    right = (r, lax.rem(t + 1, nt))
-    left = (r, lax.rem(t + nt - 1, nt))
-    half = nt // 2
-
-    def hop(which_way, h, c):
-        if which_way == 0:
-            have, there, to = (nt - (h - 1)) % nt, nt - h, right
-        else:
-            have, there, to = h - 1, h, left
-        piece = pl.ds(c * rows, rows)
-        src = f_ref.at[piece, :] if have == 0 else ring.at[have, piece, :]
-        return pltpu.make_async_remote_copy(
-            src_ref=src,
-            dst_ref=ring.at[there, piece, :],
-            send_sem=ring_send.at[which_way, h - 1, c],
-            recv_sem=ring_recv.at[there, c],
-            device_id=to,
-            device_id_type=MESH,
-        )
-
-    def hops(h):
-        if h < half:
-            return [(0, 0), (1, 0), (0, 1), (1, 1)]
-        return [(0, 0), (1, 1)]
-
-    for way, c in hops(1):
-        hop(way, 1, c).start()
-
-    @pl.loop(1, nt)
-    def _(k):
-        pltpu.make_async_remote_copy(
-            src_ref=stats.at[t],
-            dst_ref=stats.at[t],
-            send_sem=st_send,
-            recv_sem=st_recv,
-            device_id=(r, lax.rem(t + k, nt)),
-            device_id_type=MESH,
-        ).start()
-
-    @pl.loop(1, nr)
+    @pl.loop(1, nr, unroll=True)
     def _(k):
         to = lax.rem(r + k, nr)
         pltpu.make_async_remote_copy(
@@ -323,6 +323,8 @@
     cached_scores(rows // 4, rows)
     ring_stage(1, (1,))
 
+    if half > 2:
+        ring_stage(2, (0,))
     loads[1].wait()
     wait_bytes(got.at[pl.ds(0, (nr - 1) * 16), :], a2a_recv)
     arrived = got[...]
@@ -337,11 +339,10 @@
     group = 8
     part[...] = jnp.zeros(part.shape, F32)
 
-    @pl.loop(0, pool // group)
-    def _(g):
+    def low_rank(g):
         base = g * group
         block = lax.dot_general(
-            pa[pl.ds(pl.multiple_of(base * rank, group * rank), group * rank), :],
+            pa[base * rank : (base + group) * rank, :],
             x,
             NT,
             preferred_element_type=F32,
@@ -353,7 +354,12 @@
             )
         part[:, :, pl.ds(0, ntot)] += picked.reshape(nt, kpart, ntot)
 
-    @pl.loop(1, nt)
+    for g in range(pool // group):
+        low_rank(g)
+        if g == 1 and half > 2:
+            ring_stage(2, (1,))
+
+    @pl.loop(1, nt, unroll=True)
     def _(k):
         to = lax.rem(t + k, nt)
         pltpu.make_async_remote_copy(
@@ -364,9 +370,6 @@
             device_id=(r, to),
             device_id_type=MESH,
         ).start()
-
-    if half > 2:
-        ring_stage(2)
 
     qrows = 8
     span = qrows * per_row
@@ -431,7 +434,7 @@
         whole += jnp.where(k == t, 0.0, rs_got[k])
     coeff[t] = whole
 
-    @pl.loop(1, nt)
+    @pl.loop(1, nt, unroll=True)
     def _(k):
         pltpu.make_async_remote_copy(
             src_ref=coeff.at[t],
@@ -468,7 +471,7 @@
     ret_send[...] = delta[0:nvis]
     own_delta = delta[nvis:ntot]
 
-    @pl.loop(1, nr)
+    @pl.loop(1, nr, unroll=True)
     def _(k):
         to = lax.rem(r + k, nr)
         pltpu.make_async_remote_copy(

time: 39.1 us -> 41.6 us (1.064)
  Pallas kernels: 38.3 us -> 40.9 us
    pallas_call x1, Pallas kernels: 36.7 us -> 39.3 us  [shards(): pl.pallas_call(functools.partial(kernel, nr, nt), out_shape=(jax.ShapeDty...]
where the time goes in v4:
time: 41.6 us; the launch traced here: 41.5 us
  Pallas kernels  40.9 us (98%)
  between operations  0.64 us (2%)
    pallas_call x1, Pallas kernels, shards(): pl.pallas_call(functools.partial(kernel, nr, nt), out_shape=(jax.ShapeDty...  39.3 us
    pallas_call x1, Pallas kernels, shards(): pl.pallas_call(write_out, out_shape=shapes, in_specs=[vmem] * 3, out_spec...  1.61 us

profile of v4, /device:TPU:1, one launch (start us, length us, event | category | flops | bytes accessed | tf_op | source)
XLA Modules:
  0.0 41.5 jit_solution(5039262728415421947)
XLA Ops:
  0.6 39.3 %shard_map.157 = (bf16[64,1024]{1,0:T(8,128)(2,1)}, bf16[64,128]{1,0:T(8,128)(2,1)}, bf16[64,128]{1,0:T(8,128)(2,1)}) custom-call(bf16[64,1024]{1,0:T(8,128)(2,1)} %bitcast.16, bf16[8,128]{1,0:T(8,128)(2,1)} %bitcast.20, s32[1,1024]{1,0:T(1,128)} %bitcast.19, s32[16,32]{1,0:T(8,128)} %bitcast.18, s32[1,32]{1,0:T(1,128)} %bitcast.22, s32[32]{0:T(128)} %len_s_hbm.1, ...), custom_call_target="tpu_custom_call" | custom-call | flops 268435456 | bytes 12582912 | tf_op jit(solution)/shard_map/pallas_call | solution.py:594
  39.9 1.6 %shard_map.158 = (bf16[64,1024]{1,0:T(8,128)(2,1)}, bf16[64,128]{1,0:T(8,128)(2,1)}, bf16[64,128]{1,0:T(8,128)(2,1)}) custom-call(bf16[64,1024]{1,0:T(8,128)(2,1)} %get-tuple-element.9.a, bf16[64,128]{1,0:T(8,128)(2,1)} %get-tuple-element.10.b, bf16[64,128]{1,0:T(8,128)(2,1)} %get-tuple-element.11.c), custom_call_target="tpu_custom_call" | custom-call | tf_op jit(solution)/shard_map/pallas_call | solution.py:680

commit v5 on v3

--- a/solution.py
+++ b/solution.py
@@ -46,7 +46,6 @@
     att_ref,
     nk_ref,
     nv_ref,
-    f_ref,
     gain_ref,
     place_ref,
     need_ref,
@@ -100,7 +99,7 @@
 ):
     r = lax.axis_index("replica")
     t = lax.axis_index("tp")
-    rows2, width = f_ref.shape
+    rows2, width = f_hbm.shape
     rows = rows2 // 2
     need_count = need_ref.shape[0]
     adapters = place_ref.shape[1]
@@ -114,7 +113,7 @@
         pltpu.make_async_copy(a, b, small_sem.at[k])
         for k, (a, b) in enumerate(
             [
-                (f_hbm, f_ref),
+                (f_hbm, ring.at[0]),
                 (gain_hbm, gain_ref),
                 (ra_hbm, ra_ref),
                 (need_hbm, need_ref),
@@ -134,27 +133,28 @@
         pltpu.make_async_copy(pb_hbm, pb, load_sem.at[4]),
         pltpu.make_async_copy(cv_hbm, cv, load_sem.at[5]),
     ]
+
+    barrier = pltpu.get_barrier_semaphore()
+
+    @pl.loop(1, nr)
+    def _(k):
+        pl.semaphore_signal(
+            barrier, inc=1, device_id=(lax.rem(r + k, nr), t), device_id_type=MESH
+        )
+
+    @pl.loop(1, nt)
+    def _(k):
+        pl.semaphore_signal(
+            barrier, inc=1, device_id=(r, lax.rem(t + k, nt)), device_id_type=MESH
+        )
+
     for load in small + loads:
         load.start()
-
-    barrier = pltpu.get_barrier_semaphore()
-
-    @pl.loop(1, nr)
-    def _(k):
-        pl.semaphore_signal(
-            barrier, inc=1, device_id=(lax.rem(r + k, nr), t), device_id_type=MESH
-        )
-
-    @pl.loop(1, nt)
-    def _(k):
-        pl.semaphore_signal(
-            barrier, inc=1, device_id=(r, lax.rem(t + k, nt)), device_id_type=MESH
-        )
 
     small[0].wait()
     small[1].wait()
     gain_rows = gain_ref[...].astype(F32)
-    f32 = f_ref[...].astype(F32)
+    f32 = ring[0].astype(F32)
     lanes = HD
     chunks = width // lanes
     eye = iota((rows2, lanes), 0) == iota((rows2, lanes), 1)
@@ -184,11 +184,10 @@
     place = place_ref[...]
     home = place // pool
     local = place - home * pool
-    at_me = jnp.where(home == r, local + 1, 0)
     table = jnp.concatenate(
         [
             jnp.broadcast_to(x.astype(F32), (8, adapters))
-            for x in (home, local, at_me)
+            for x in (home, local)
         ],
         axis=0,
     ).astype(BF16)
@@ -230,9 +229,8 @@
         else:
             have, there, to = h - 1, h, left
         piece = pl.ds(c * rows, rows)
-        src = f_ref.at[piece, :] if have == 0 else ring.at[have, piece, :]
         return pltpu.make_async_remote_copy(
-            src_ref=src,
+            src_ref=ring.at[have, piece, :],
             dst_ref=ring.at[there, piece, :],
             send_sem=ring_send.at[which_way, h - 1, c],
             recv_sem=ring_recv.at[there, c],
@@ -274,14 +272,34 @@
     def wait_bytes(ref, sem):
         pltpu.make_async_copy(ref, ref, sem).wait()
 
-    asked = jnp.zeros((adapters, nr), jnp.bool_)
-    p_iota = iota((adapters, nr), 0)
-    for e in range(need_count):
-        asked = asked | (p_iota == need[e : e + 1, :])
-    visit = jnp.dot(
-        table, jnp.where(asked, 1.0, 0.0).astype(BF16), preferred_element_type=F32
-    )[16:24]
-    spread = jnp.where(iota((nr, nvis), 1) // 4 == iota((nr, nvis), 0), 1.0, 0.0)
+    packs = max(1, min(HD // nr, need_count))
+    while need_count % packs:
+        packs -= 1
+    tall = need_count // packs
+    packed = jnp.concatenate(
+        [need[k * tall : (k + 1) * tall, :] for k in range(packs)], axis=1
+    )
+    span_p = 256
+
+    def visitors(k, total):
+        base = pl.multiple_of(k * span_p, span_p)
+        p_iota = iota((span_p, packs * nr), 0) + base
+        asked = p_iota == packed[0:1, :]
+        for e in range(1, tall):
+            asked = asked | (p_iota == packed[e : e + 1, :])
+        there = place_ref[:, pl.ds(base, span_p)]
+        there_home = there // pool
+        slot1 = jnp.where(there_home == r, there - there_home * pool + 1, 0)
+        slot1 = jnp.broadcast_to(slot1.astype(F32), (8, span_p)).astype(BF16)
+        return total + jnp.dot(
+            slot1, jnp.where(asked, 1.0, 0.0).astype(BF16), preferred_element_type=F32
+        )
+
+    visit = lax.fori_loop(
+        0, adapters // span_p, visitors, jnp.zeros((8, packs * nr), F32)
+    )
+    wide = (packs * nr, nvis)
+    spread = jnp.where(iota(wide, 1) // 4 == iota(wide, 0) % nr, 1.0, 0.0)
     visit_slot = jnp.dot(
         visit.astype(BF16), spread.astype(BF16), preferred_element_type=F32
     )[0:1].astype(jnp.int32) - 1
@@ -293,7 +311,7 @@
     per_row = 2 * GROUP
 
     def cached_scores(lo, hi):
-        @pl.loop(lo, hi, unroll=4)
+        @pl.loop(lo, hi, unroll=2)
         def _(i):
             s = (
                 lax.dot_general(q_ref[i], ck[i], NT, preferred_element_type=F32) * scale
@@ -323,6 +341,8 @@
     cached_scores(rows // 4, rows)
     ring_stage(1, (1,))
 
+    if half > 2:
+        ring_stage(2, (0,))
     loads[1].wait()
     wait_bytes(got.at[pl.ds(0, (nr - 1) * 16), :], a2a_recv)
     arrived = got[...]
@@ -334,7 +354,7 @@
             preferred_element_type=F32,
         ).astype(BF16)
     x = xall[...]
-    group = 8
+    group = 4
     part[...] = jnp.zeros(part.shape, F32)
 
     @pl.loop(0, pool // group)
@@ -366,21 +386,20 @@
         ).start()
 
     if half > 2:
-        ring_stage(2)
+        ring_stage(2, (1,))
 
     qrows = 8
     span = qrows * per_row
-    for b in range(rows // qrows):
-        s = scores[b * qrows : (b + 1) * qrows].reshape(span, cache_len)
+    @pl.loop(0, rows // qrows)
+    def _(b):
+        group_rows = pl.ds(b * qrows, qrows)
+        lines = pl.ds(pl.multiple_of(b * span, span), span)
+        s = scores[group_rows].reshape(span, cache_len)
         top = jnp.max(s, axis=1, keepdims=True)
         e_cache = jnp.exp(s - top)
-        top_ref[b * span : (b + 1) * span, :] = top
-        bottom_ref[b * span : (b + 1) * span, :] = jnp.sum(
-            e_cache, axis=1, keepdims=True
-        )
-        weights[b * qrows : (b + 1) * qrows] = e_cache.astype(BF16).reshape(
-            qrows, per_row, cache_len
-        )
+        top_ref[lines, :] = top
+        bottom_ref[lines, :] = jnp.sum(e_cache, axis=1, keepdims=True)
+        weights[group_rows] = e_cache.astype(BF16).reshape(qrows, per_row, cache_len)
 
     wait_bytes(stats.at[pl.ds(0, nt - 1)], st_recv)
     square = stats[0, 8:16, :]
@@ -389,11 +408,12 @@
     inverse_row = lax.rsqrt(square[0:1] / (width * nt) + EPS)
     inverse = jnp.sum(jnp.where(eye, inverse_row, 0.0), axis=1, keepdims=True)
 
+    acc_kv[...] = jnp.zeros(acc_kv.shape, F32)
+
     def project(o):
         source = lax.rem(t + o, nt)
-        block = f_ref[...] if o == 0 else ring[o]
-        block = block.astype(F32) * inverse
-        gains = stats[source][0:8]
+        block = ring[o].astype(F32) * inverse
+        gains = stats[source, 0:8, :]
         normed = jnp.concatenate(
             [
                 block[:, c * lanes : (c + 1) * lanes] * gains[c : c + 1]
@@ -402,18 +422,16 @@
             axis=1,
         ).astype(BF16)
         w = wbuf[pl.ds(pl.multiple_of(source * width, width), width), :]
-        product = jnp.dot(normed, w, preferred_element_type=F32)
-        if o == 0:
-            acc_kv[...] = product
-        else:
-            acc_kv[...] += product
+        acc_kv[...] += jnp.dot(normed, w, preferred_element_type=F32)
+
+    def project_all(first, count, stride):
+        @pl.loop(0, count)
+        def _(k):
+            project(lax.rem(first + k * stride, nt))
 
     loads[2].wait()
     loads[3].wait()
-    project(0)
-    project(nt - 1)
-    if half > 1:
-        project(1)
+    project_all(nt - 1, 3, 1)
 
     length_row = len_ref[...].astype(F32)
     positions = jnp.sum(
@@ -422,8 +440,15 @@
     positions = jnp.concatenate([positions, positions + 1.0], axis=0)
     angle = positions * freq_ref[...]
     sign = jnp.where(iota((rows2, HD), 1) < HD // 2, -1.0, 1.0)
-    cos_ref[...] = jnp.cos(angle)
-    sin_ref[...] = jnp.sin(angle) * sign
+    cos_ref[...] = angle
+    sin_ref[...] = sign
+
+    @pl.loop(0, rows2 // 8)
+    def _(k):
+        lines = pl.ds(pl.multiple_of(k * 8, 8), 8)
+        some = cos_ref[lines, :]
+        cos_ref[lines, :] = jnp.cos(some)
+        sin_ref[lines, :] = jnp.sin(some) * sin_ref[lines, :]
 
     wait_bytes(rs_got.at[pl.ds(0, nt - 1)], rs_recv)
     whole = part[t]
@@ -444,26 +469,31 @@
 
     for h in range(3, half):
         ring_stage(h)
-        project(nt - h + 1)
-        project(h - 1)
+        project_all(nt - h + 1, 2, 2 * (h - 1))
 
     loads[5].wait()
 
-    @pl.loop(0, rows, unroll=4)
+    @pl.loop(0, rows, unroll=2)
     def _(i):
         att_acc[pl.ds(pl.multiple_of(i * per_row, per_row), per_row), :] = jnp.dot(
             weights[i], cv[i], preferred_element_type=F32
         )
 
     loads[4].wait()
-    pbt[...] = pb[...].T
+
+    @pl.loop(0, pool * rank // HD)
+    def _(k):
+        lines = pl.ds(pl.multiple_of(k * HD, HD), HD)
+        pbt[:, lines] = pb[lines, :].T
 
     wait_bytes(coeff.at[pl.ds(0, nt - 1)], ag_recv)
     coeffs = coeff[...].reshape(rank, coeff.shape[2])[:, 0:ntot]
-    for s in range(pool):
-        expand[s * rank : (s + 1) * rank, :] = jnp.where(
+    @pl.loop(0, pool)
+    def _(s):
+        expand[pl.ds(pl.multiple_of(s * rank, rank), rank), :] = jnp.where(
             slot_row == s, coeffs, 0.0
         ).astype(BF16)
+
     delta = jnp.dot(pbt[...], expand[...], preferred_element_type=F32).T
     ret_send[...] = delta[0:nvis]
     own_delta = delta[nvis:ntot]
@@ -480,20 +510,18 @@
             device_id_type=MESH,
         ).start()
 
-    if half > 2:
-        project(nt - half + 1)
-        project(half - 1)
     ring_stage(half)
-    project(half)
+    project_all(half - 1, 3, 1)
 
     key = acc_kv[:, 0:HD]
     turned = key * cos_ref[...] + pltpu.roll(key, HD // 2, 1) * sin_ref[...]
     new_keys = turned.astype(BF16)
     nk_ref[...] = new_keys
 
-    for b in range(rows // qrows):
-        part_rows = slice(b * span, (b + 1) * span)
-        q = q_ref[b * qrows : (b + 1) * qrows].reshape(span, HD)
+    @pl.loop(0, rows // qrows)
+    def _(b):
+        part_rows = pl.ds(pl.multiple_of(b * span, span), span)
+        q = q_ref[pl.ds(b * qrows, qrows)].reshape(span, HD)
         fresh = (
             lax.dot_general(q, new_keys, NT, preferred_element_type=F32) * scale
         )
@@ -598,7 +626,6 @@
         in_specs=[hbm] * 15,
         out_specs=(vmem, vmem, vmem),
         scratch_shapes=[
-            pltpu.VMEM((rows2, width), BF16),
             pltpu.VMEM((width // HD, HD), BF16),
             pltpu.VMEM((1, placement.shape[0]), jnp.int32),
             pltpu.VMEM(need_lists.shape[::-1], jnp.int32),

time: 39.1 us -> 41.9 us (1.072)
  Pallas kernels: 38.3 us -> 41.1 us
    pallas_call x1, Pallas kernels: 36.7 us -> 39.5 us  [shards(): pl.pallas_call(functools.partial(kernel, nr, nt), out_shape=(jax.ShapeDty...]
where the time goes in v5:
time: 41.9 us; the launch traced here: 41.8 us
  Pallas kernels  41.1 us (98%)
  between operations  0.64 us (2%)
    pallas_call x1, Pallas kernels, shards(): pl.pallas_call(functools.partial(kernel, nr, nt), out_shape=(jax.ShapeDty...  39.5 us
    pallas_call x1, Pallas kernels, shards(): pl.pallas_call(write_out, out_shape=shapes, in_specs=[vmem] * 3, out_spec...  1.61 us

profile of v5, /device:TPU:1, one launch (start us, length us, event | category | flops | bytes accessed | tf_op | source)
XLA Modules:
  0.0 41.8 jit_solution(933441663121870691)
XLA Ops:
  0.6 39.5 %shard_map.157 = (bf16[64,1024]{1,0:T(8,128)(2,1)}, bf16[64,128]{1,0:T(8,128)(2,1)}, bf16[64,128]{1,0:T(8,128)(2,1)}) custom-call(bf16[64,1024]{1,0:T(8,128)(2,1)} %bitcast.16, bf16[8,128]{1,0:T(8,128)(2,1)} %bitcast.20, s32[1,1024]{1,0:T(1,128)} %bitcast.19, s32[16,32]{1,0:T(8,128)} %bitcast.18, s32[1,32]{1,0:T(1,128)} %bitcast.22, s32[32]{0:T(128)} %len_s_hbm.1, ...), custom_call_target="tpu_custom_call" | custom-call | flops 268435456 | bytes 12582912 | tf_op jit(solution)/shard_map/pallas_call | solution.py:619
  40.2 1.6 %shard_map.158 = (bf16[64,1024]{1,0:T(8,128)(2,1)}, bf16[64,128]{1,0:T(8,128)(2,1)}, bf16[64,128]{1,0:T(8,128)(2,1)}) custom-call(bf16[64,1024]{1,0:T(8,128)(2,1)} %get-tuple-element.9.a, bf16[64,128]{1,0:T(8,128)(2,1)} %get-tuple-element.10.b, bf16[64,128]{1,0:T(8,128)(2,1)} %get-tuple-element.11.c), custom_call_target="tpu_custom_call" | custom-call | tf_op jit(solution)/shard_map/pallas_call | solution.py:704

commit v6 on v3

--- a/solution.py
+++ b/solution.py
@@ -17,7 +17,7 @@
 MESH = pl.DeviceIdType.MESH
 F32 = jnp.float32
 BF16 = jnp.bfloat16
-QUARTER = 256
+SENT = 32
 NT = (((1,), (1,)), ((), ()))
 
 
@@ -65,6 +65,7 @@
     cv,
     stats,
     msg,
+    wide_rows,
     got,
     xall,
     ring,
@@ -114,11 +115,11 @@
         pltpu.make_async_copy(a, b, small_sem.at[k])
         for k, (a, b) in enumerate(
             [
-                (f_hbm, f_ref),
-                (gain_hbm, gain_ref),
                 (ra_hbm, ra_ref),
                 (need_hbm, need_ref),
                 (place_hbm, place_ref),
+                (gain_hbm, gain_ref),
+                (f_hbm, f_ref),
                 (len_s_hbm, len_s),
                 (len_hbm, len_ref),
                 (freq_hbm, freq_ref),
@@ -134,7 +135,7 @@
         pltpu.make_async_copy(pb_hbm, pb, load_sem.at[4]),
         pltpu.make_async_copy(cv_hbm, cv, load_sem.at[5]),
     ]
-    for load in small + loads:
+    for load in small:
         load.start()
 
     barrier = pltpu.get_barrier_semaphore()
@@ -151,28 +152,10 @@
             barrier, inc=1, device_id=(r, lax.rem(t + k, nt)), device_id_type=MESH
         )
 
-    small[0].wait()
-    small[1].wait()
-    gain_rows = gain_ref[...].astype(F32)
-    f32 = f_ref[...].astype(F32)
-    lanes = HD
-    chunks = width // lanes
-    eye = iota((rows2, lanes), 0) == iota((rows2, lanes), 1)
-    square_sum = jnp.sum(f32 * f32, axis=1, keepdims=True)
-    square_row = jnp.sum(jnp.where(eye, square_sum, 0.0), axis=0, keepdims=True)
-    stats[t] = jnp.concatenate(
-        [gain_rows, jnp.broadcast_to(square_row, (8, lanes))], axis=0
-    )
-    own = jnp.concatenate(
-        [
-            f32[:, c * lanes : (c + 1) * lanes] * gain_rows[c : c + 1]
-            for c in range(chunks)
-        ],
-        axis=1,
-    ).astype(BF16)
-    xall[pl.ds(nvis, rows2), :] = own
-
-    for load in small[2:5]:
+    for load in loads:
+        load.start()
+
+    for load in small[:3]:
         load.wait()
     ra = ra_ref[...]
     need = need_ref[...]
@@ -203,19 +186,38 @@
     twin = (ra_col == ra_f) & (iota((rows, rows), 0) < iota((rows, rows), 1))
     turn = jnp.sum(jnp.where(twin, 1.0, 0.0), axis=0, keepdims=True).astype(jnp.int32)
     is_far = ra < need_count
-    code = jnp.where(is_far, owner * 16 + turn * 8, -1000)
-    code2 = jnp.concatenate([code, code + 4], axis=1)
-
-    slot_iota = iota((nr * 16, rows2), 0)
-    total = None
-    for j in range(4):
-        pick = jnp.where(slot_iota == code2 + j, 1.0, 0.0).astype(BF16)
-        piece = jnp.dot(
-            pick, own[:, j * QUARTER : (j + 1) * QUARTER], preferred_element_type=F32
-        )
-        total = piece if total is None else total + piece
-    msg[...] = total.astype(BF16)
-    got[pl.ds(pl.multiple_of(r * 16, 16), 16), :] = jnp.zeros((16, QUARTER), BF16)
+    code = jnp.where(is_far, owner * 4 + turn * 2, -1000)
+    code2 = jnp.concatenate([code, code + 1], axis=1)
+    pick = jnp.where(iota((nvis, rows2), 0) == code2, 1.0, 0.0).astype(BF16)
+
+    small[3].wait()
+    small[4].wait()
+    gain_rows = gain_ref[...].astype(F32)
+    f32 = f_ref[...].astype(F32)
+    lanes = HD
+    chunks = width // lanes
+    eye = iota((rows2, lanes), 0) == iota((rows2, lanes), 1)
+    square_sum = jnp.sum(f32 * f32, axis=1, keepdims=True)
+    square_row = jnp.sum(jnp.where(eye, square_sum, 0.0), axis=0, keepdims=True)
+    stats[t] = jnp.concatenate(
+        [gain_rows, jnp.broadcast_to(square_row, (8, lanes))], axis=0
+    )
+    own = jnp.concatenate(
+        [
+            f32[:, c * lanes : (c + 1) * lanes] * gain_rows[c : c + 1]
+            for c in range(chunks)
+        ],
+        axis=1,
+    ).astype(BF16)
+    xall[pl.ds(nvis, rows2), :] = own
+
+    picked_rows = jnp.dot(pick, own, preferred_element_type=F32)
+    for j in range(chunks):
+        wide_rows[pl.ds(j, nvis, stride=chunks), :] = picked_rows[
+            :, j * lanes : (j + 1) * lanes
+        ]
+    msg[...] = wide_rows[...].astype(BF16)
+    got[pl.ds(pl.multiple_of(r * SENT, SENT), SENT), :] = jnp.zeros((SENT, HD), BF16)
     ret_got[pl.ds(pl.multiple_of(r * 8, 8), 8), :] = jnp.zeros((8, HD), F32)
 
     pl.semaphore_wait(barrier, nr - 1 + nt - 1)
@@ -245,6 +247,18 @@
             return [(0, 0), (1, 0), (0, 1), (1, 1)]
         return [(0, 0), (1, 1)]
 
+    @pl.loop(1, nr)
+    def _(k):
+        to = lax.rem(r + k, nr)
+        pltpu.make_async_remote_copy(
+            src_ref=msg.at[pl.ds(pl.multiple_of(to * SENT, SENT), SENT), :],
+            dst_ref=got.at[pl.ds(pl.multiple_of(r * SENT, SENT), SENT), :],
+            send_sem=a2a_send,
+            recv_sem=a2a_recv,
+            device_id=(to, t),
+            device_id_type=MESH,
+        ).start()
+
     for way, c in hops(1):
         hop(way, 1, c).start()
 
@@ -256,18 +270,6 @@
             send_sem=st_send,
             recv_sem=st_recv,
             device_id=(r, lax.rem(t + k, nt)),
-            device_id_type=MESH,
-        ).start()
-
-    @pl.loop(1, nr)
-    def _(k):
-        to = lax.rem(r + k, nr)
-        pltpu.make_async_remote_copy(
-            src_ref=msg.at[pl.ds(pl.multiple_of(to * 16, 16), 16), :],
-            dst_ref=got.at[pl.ds(pl.multiple_of(r * 16, 16), 16), :],
-            send_sem=a2a_send,
-            recv_sem=a2a_recv,
-            device_id=(to, t),
             device_id_type=MESH,
         ).start()
 
@@ -320,19 +322,16 @@
     loads[0].wait()
     cached_scores(0, rows // 4)
     ring_stage(1, (0,))
-    cached_scores(rows // 4, rows)
+    cached_scores(rows // 4, rows // 2)
     ring_stage(1, (1,))
 
     loads[1].wait()
-    wait_bytes(got.at[pl.ds(0, (nr - 1) * 16), :], a2a_recv)
-    arrived = got[...]
-    for j in range(4):
-        gather = iota((nvis, nr * 16), 1) == iota((nvis, nr * 16), 0) * 4 + j
-        xall[pl.ds(0, nvis), j * QUARTER : (j + 1) * QUARTER] = jnp.dot(
-            jnp.where(gather, 1.0, 0.0).astype(BF16),
-            arrived,
-            preferred_element_type=F32,
-        ).astype(BF16)
+    wait_bytes(got.at[pl.ds(0, (nr - 1) * SENT), :], a2a_recv)
+    wide_rows[...] = got[...].astype(F32)
+    for j in range(chunks):
+        xall[pl.ds(0, nvis), j * lanes : (j + 1) * lanes] = wide_rows[
+            pl.ds(j, nvis, stride=chunks), :
+        ].astype(BF16)
     x = xall[...]
     group = 8
     part[...] = jnp.zeros(part.shape, F32)
@@ -365,8 +364,7 @@
             device_id_type=MESH,
         ).start()
 
-    if half > 2:
-        ring_stage(2)
+    cached_scores(rows // 2, rows)
 
     qrows = 8
     span = qrows * per_row
@@ -381,6 +379,26 @@
         weights[b * qrows : (b + 1) * qrows] = e_cache.astype(BF16).reshape(
             qrows, per_row, cache_len
         )
+
+    wait_bytes(rs_got.at[pl.ds(0, nt - 1)], rs_recv)
+    whole = part[t]
+    for k in range(nt):
+        whole += jnp.where(k == t, 0.0, rs_got[k])
+    coeff[t] = whole
+
+    @pl.loop(1, nt)
+    def _(k):
+        pltpu.make_async_remote_copy(
+            src_ref=coeff.at[t],
+            dst_ref=coeff.at[t],
+            send_sem=ag_send,
+            recv_sem=ag_recv,
+            device_id=(r, lax.rem(t + k, nt)),
+            device_id_type=MESH,
+        ).start()
+
+    if half > 2:
+        ring_stage(2)
 
     wait_bytes(stats.at[pl.ds(0, nt - 1)], st_recv)
     square = stats[0, 8:16, :]
@@ -425,36 +443,6 @@
     cos_ref[...] = jnp.cos(angle)
     sin_ref[...] = jnp.sin(angle) * sign
 
-    wait_bytes(rs_got.at[pl.ds(0, nt - 1)], rs_recv)
-    whole = part[t]
-    for k in range(nt):
-        whole += jnp.where(k == t, 0.0, rs_got[k])
-    coeff[t] = whole
-
-    @pl.loop(1, nt)
-    def _(k):
-        pltpu.make_async_remote_copy(
-            src_ref=coeff.at[t],
-            dst_ref=coeff.at[t],
-            send_sem=ag_send,
-            recv_sem=ag_recv,
-            device_id=(r, lax.rem(t + k, nt)),
-            device_id_type=MESH,
-        ).start()
-
-    for h in range(3, half):
-        ring_stage(h)
-        project(nt - h + 1)
-        project(h - 1)
-
-    loads[5].wait()
-
-    @pl.loop(0, rows, unroll=4)
-    def _(i):
-        att_acc[pl.ds(pl.multiple_of(i * per_row, per_row), per_row), :] = jnp.dot(
-            weights[i], cv[i], preferred_element_type=F32
-        )
-
     loads[4].wait()
     pbt[...] = pb[...].T
 
@@ -479,6 +467,19 @@
             device_id=(to, t),
             device_id_type=MESH,
         ).start()
+
+    for h in range(3, half):
+        ring_stage(h)
+        project(nt - h + 1)
+        project(h - 1)
+
+    loads[5].wait()
+
+    @pl.loop(0, rows, unroll=4)
+    def _(i):
+        att_acc[pl.ds(pl.multiple_of(i * per_row, per_row), per_row), :] = jnp.dot(
+            weights[i], cv[i], preferred_element_type=F32
+        )
 
     if half > 2:
         project(nt - half + 1)
@@ -541,7 +542,7 @@
         for way, c in hops(h):
             hop(way, h, c).wait_send()
     wait_bytes(stats.at[pl.ds(0, nt - 1)], st_send)
-    wait_bytes(msg.at[pl.ds(0, (nr - 1) * 16), :], a2a_send)
+    wait_bytes(msg.at[pl.ds(0, (nr - 1) * SENT), :], a2a_send)
     wait_bytes(part.at[pl.ds(0, nt - 1)], rs_send)
     wait_bytes(coeff.at[pl.ds(0, nt - 1)], ag_send)
     wait_bytes(ret_got.at[pl.ds(0, (nr - 1) * 8), :], re_send)
@@ -616,8 +617,9 @@
             pltpu.VMEM((rows, cache_len, HD), BF16),
             pltpu.VMEM((rows, cache_len, HD), BF16),
             pltpu.VMEM((nt, 16, HD), F32),
-            pltpu.VMEM((nr * 16, QUARTER), BF16),
-            pltpu.VMEM((nr * 16, QUARTER), BF16),
+            pltpu.VMEM((nr * SENT, HD), BF16),
+            pltpu.VMEM((nr * SENT, HD), F32),
+            pltpu.VMEM((nr * SENT, HD), BF16),
             pltpu.VMEM((ntot, width), BF16),
             pltpu.VMEM((nt, rows2, width), BF16),
             pltpu.VMEM((nt, rank // nt, ntot_pad), F32),

time: 39.1 us -> 38.5 us (0.985)
  Pallas kernels: 38.3 us -> 37.7 us
    pallas_call x1, Pallas kernels: 36.7 us -> 36.1 us  [shards(): pl.pallas_call(functools.partial(kernel, nr, nt), out_shape=(jax.ShapeDty...]
where the time goes in v6:
time: 38.5 us; the launch traced here: 38.4 us
  Pallas kernels  37.7 us (98%)
  between operations  0.64 us (2%)
    pallas_call x1, Pallas kernels, shards(): pl.pallas_call(functools.partial(kernel, nr, nt), out_shape=(jax.ShapeDty...  36.1 us
    pallas_call x1, Pallas kernels, shards(): pl.pallas_call(write_out, out_shape=shapes, in_specs=[vmem] * 3, out_spec...  1.61 us

profile of v6, /device:TPU:1, one launch (start us, length us, event | category | flops | bytes accessed | tf_op | source)
XLA Modules:
  0.0 38.4 jit_solution(7037437372790400537)
XLA Ops:
  0.6 36.1 %shard_map.157 = (bf16[64,1024]{1,0:T(8,128)(2,1)}, bf16[64,128]{1,0:T(8,128)(2,1)}, bf16[64,128]{1,0:T(8,128)(2,1)}) custom-call(bf16[64,1024]{1,0:T(8,128)(2,1)} %bitcast.16, bf16[8,128]{1,0:T(8,128)(2,1)} %bitcast.20, s32[1,1024]{1,0:T(1,128)} %bitcast.19, s32[16,32]{1,0:T(8,128)} %bitcast.18, s32[1,32]{1,0:T(1,128)} %bitcast.22, s32[32]{0:T(128)} %len_s_hbm.1, ...), custom_call_target="tpu_custom_call" | custom-call | flops 268435456 | bytes 12582912 | tf_op jit(solution)/shard_map/pallas_call | solution.py:592
  36.8 1.6 %shard_map.158 = (bf16[64,1024]{1,0:T(8,128)(2,1)}, bf16[64,128]{1,0:T(8,128)(2,1)}, bf16[64,128]{1,0:T(8,128)(2,1)}) custom-call(bf16[64,1024]{1,0:T(8,128)(2,1)} %get-tuple-element.9.a, bf16[64,128]{1,0:T(8,128)(2,1)} %get-tuple-element.10.b, bf16[64,128]{1,0:T(8,128)(2,1)} %get-tuple-element.11.c), custom_call_target="tpu_custom_call" | custom-call | tf_op jit(solution)/shard_map/pallas_call | solution.py:679

commit v7 on v6

--- a/solution.py
+++ b/solution.py
@@ -192,36 +192,7 @@
 
     small[3].wait()
     small[4].wait()
-    gain_rows = gain_ref[...].astype(F32)
-    f32 = f_ref[...].astype(F32)
-    lanes = HD
-    chunks = width // lanes
-    eye = iota((rows2, lanes), 0) == iota((rows2, lanes), 1)
-    square_sum = jnp.sum(f32 * f32, axis=1, keepdims=True)
-    square_row = jnp.sum(jnp.where(eye, square_sum, 0.0), axis=0, keepdims=True)
-    stats[t] = jnp.concatenate(
-        [gain_rows, jnp.broadcast_to(square_row, (8, lanes))], axis=0
-    )
-    own = jnp.concatenate(
-        [
-            f32[:, c * lanes : (c + 1) * lanes] * gain_rows[c : c + 1]
-            for c in range(chunks)
-        ],
-        axis=1,
-    ).astype(BF16)
-    xall[pl.ds(nvis, rows2), :] = own
-
-    picked_rows = jnp.dot(pick, own, preferred_element_type=F32)
-    for j in range(chunks):
-        wide_rows[pl.ds(j, nvis, stride=chunks), :] = picked_rows[
-            :, j * lanes : (j + 1) * lanes
-        ]
-    msg[...] = wide_rows[...].astype(BF16)
-    got[pl.ds(pl.multiple_of(r * SENT, SENT), SENT), :] = jnp.zeros((SENT, HD), BF16)
-    ret_got[pl.ds(pl.multiple_of(r * 8, 8), 8), :] = jnp.zeros((8, HD), F32)
-
     pl.semaphore_wait(barrier, nr - 1 + nt - 1)
-
     right = (r, lax.rem(t + 1, nt))
     left = (r, lax.rem(t + nt - 1, nt))
     half = nt // 2
@@ -247,6 +218,37 @@
             return [(0, 0), (1, 0), (0, 1), (1, 1)]
         return [(0, 0), (1, 1)]
 
+    for way, c in hops(1):
+        hop(way, 1, c).start()
+
+    gain_rows = gain_ref[...].astype(F32)
+    f32 = f_ref[...].astype(F32)
+    lanes = HD
+    chunks = width // lanes
+    eye = iota((rows2, lanes), 0) == iota((rows2, lanes), 1)
+    square_sum = jnp.sum(f32 * f32, axis=1, keepdims=True)
+    square_row = jnp.sum(jnp.where(eye, square_sum, 0.0), axis=0, keepdims=True)
+    stats[t] = jnp.concatenate(
+        [gain_rows, jnp.broadcast_to(square_row, (8, lanes))], axis=0
+    )
+    own = jnp.concatenate(
+        [
+            f32[:, c * lanes : (c + 1) * lanes] * gain_rows[c : c + 1]
+            for c in range(chunks)
+        ],
+        axis=1,
+    ).astype(BF16)
+    xall[pl.ds(nvis, rows2), :] = own
+
+    picked_rows = jnp.dot(pick, own, preferred_element_type=F32)
+    for j in range(chunks):
+        wide_rows[pl.ds(j, nvis, stride=chunks), :] = picked_rows[
+            :, j * lanes : (j + 1) * lanes
+        ]
+    msg[...] = wide_rows[...].astype(BF16)
+    got[pl.ds(pl.multiple_of(r * SENT, SENT), SENT), :] = jnp.zeros((SENT, HD), BF16)
+    ret_got[pl.ds(pl.multiple_of(r * 8, 8), 8), :] = jnp.zeros((8, HD), F32)
+
     @pl.loop(1, nr)
     def _(k):
         to = lax.rem(r + k, nr)
@@ -258,9 +260,6 @@
             device_id=(to, t),
             device_id_type=MESH,
         ).start()
-
-    for way, c in hops(1):
-        hop(way, 1, c).start()
 
     @pl.loop(1, nt)
     def _(k):
@@ -364,6 +363,8 @@
             device_id_type=MESH,
         ).start()
 
+    if half > 2:
+        ring_stage(2, (0,))
     cached_scores(rows // 2, rows)
 
     qrows = 8
@@ -379,6 +380,9 @@
         weights[b * qrows : (b + 1) * qrows] = e_cache.astype(BF16).reshape(
             qrows, per_row, cache_len
         )
+
+    if half > 2:
+        ring_stage(2, (1,))
 
     wait_bytes(rs_got.at[pl.ds(0, nt - 1)], rs_recv)
     whole = part[t]
@@ -396,9 +400,6 @@
             device_id=(r, lax.rem(t + k, nt)),
             device_id_type=MESH,
         ).start()
-
-    if half > 2:
-        ring_stage(2)
 
     wait_bytes(stats.at[pl.ds(0, nt - 1)], st_recv)
     square = stats[0, 8:16, :]
@@ -446,6 +447,11 @@
     loads[4].wait()
     pbt[...] = pb[...].T
 
+    for h in range(3, half):
+        ring_stage(h)
+        project(nt - h + 1)
+        project(h - 1)
+
     wait_bytes(coeff.at[pl.ds(0, nt - 1)], ag_recv)
     coeffs = coeff[...].reshape(rank, coeff.shape[2])[:, 0:ntot]
     for s in range(pool):
@@ -467,11 +473,6 @@
             device_id=(to, t),
             device_id_type=MESH,
         ).start()
-
-    for h in range(3, half):
-        ring_stage(h)
-        project(nt - h + 1)
-        project(h - 1)
 
     loads[5].wait()
 

time: 38.5 us -> 39 us (1.013)
  Pallas kernels: 37.7 us -> 38.3 us
    pallas_call x1, Pallas kernels: 36.1 us -> 36.7 us  [shards(): pl.pallas_call(functools.partial(kernel, nr, nt), out_shape=(jax.ShapeDty...]
where the time goes in v7:
time: 39 us; the launch traced here: 38.9 us
  Pallas kernels  38.3 us (98%)
  between operations  0.64 us (2%)
    pallas_call x1, Pallas kernels, shards(): pl.pallas_call(functools.partial(kernel, nr, nt), out_shape=(jax.ShapeDty...  36.7 us
    pallas_call x1, Pallas kernels, shards(): pl.pallas_call(write_out, out_shape=shapes, in_specs=[vmem] * 3, out_spec...  1.61 us

profile of v7, /device:TPU:1, one launch (start us, length us, event | category | flops | bytes accessed | tf_op | source)
XLA Modules:
  0.0 38.9 jit_solution(11192068142680409625)
XLA Ops:
  0.6 36.7 %shard_map.157 = (bf16[64,1024]{1,0:T(8,128)(2,1)}, bf16[64,128]{1,0:T(8,128)(2,1)}, bf16[64,128]{1,0:T(8,128)(2,1)}) custom-call(bf16[64,1024]{1,0:T(8,128)(2,1)} %bitcast.16, bf16[8,128]{1,0:T(8,128)(2,1)} %bitcast.20, s32[1,1024]{1,0:T(1,128)} %bitcast.19, s32[16,32]{1,0:T(8,128)} %bitcast.18, s32[1,32]{1,0:T(1,128)} %bitcast.22, s32[32]{0:T(128)} %len_s_hbm.1, ...), custom_call_target="tpu_custom_call" | custom-call | flops 268435456 | bytes 12582912 | tf_op jit(solution)/shard_map/pallas_call | solution.py:593
  37.3 1.6 %shard_map.158 = (bf16[64,1024]{1,0:T(8,128)(2,1)}, bf16[64,128]{1,0:T(8,128)(2,1)}, bf16[64,128]{1,0:T(8,128)(2,1)}) custom-call(bf16[64,1024]{1,0:T(8,128)(2,1)} %get-tuple-element.9.a, bf16[64,128]{1,0:T(8,128)(2,1)} %get-tuple-element.10.b, bf16[64,128]{1,0:T(8,128)(2,1)} %get-tuple-element.11.c), custom_call_target="tpu_custom_call" | custom-call | tf_op jit(solution)/shard_map/pallas_call | solution.py:680

commit v8 on v7

--- a/solution.py
+++ b/solution.py
@@ -110,6 +110,7 @@
     kpart = rank // nt
     nvis = nr * 4
     ntot = nvis + rows2
+    ntot_pad = part.shape[2]
 
     small = [
         pltpu.make_async_copy(a, b, small_sem.at[k])
@@ -275,14 +276,22 @@
     def wait_bytes(ref, sem):
         pltpu.make_async_copy(ref, ref, sem).wait()
 
-    asked = jnp.zeros((adapters, nr), jnp.bool_)
-    p_iota = iota((adapters, nr), 0)
-    for e in range(need_count):
-        asked = asked | (p_iota == need[e : e + 1, :])
+    packs = max(1, min(HD // nr, need_count))
+    while need_count % packs:
+        packs -= 1
+    tall = need_count // packs
+    packed = jnp.concatenate(
+        [need[k * tall : (k + 1) * tall, :] for k in range(packs)], axis=1
+    )
+    p_iota = iota((adapters, packs * nr), 0)
+    asked = p_iota == packed[0:1, :]
+    for e in range(1, tall):
+        asked = asked | (p_iota == packed[e : e + 1, :])
     visit = jnp.dot(
         table, jnp.where(asked, 1.0, 0.0).astype(BF16), preferred_element_type=F32
     )[16:24]
-    spread = jnp.where(iota((nr, nvis), 1) // 4 == iota((nr, nvis), 0), 1.0, 0.0)
+    wide = (packs * nr, nvis)
+    spread = jnp.where(iota(wide, 1) // 4 == iota(wide, 0) % nr, 1.0, 0.0)
     visit_slot = jnp.dot(
         visit.astype(BF16), spread.astype(BF16), preferred_element_type=F32
     )[0:1].astype(jnp.int32) - 1
@@ -294,7 +303,7 @@
     per_row = 2 * GROUP
 
     def cached_scores(lo, hi):
-        @pl.loop(lo, hi, unroll=4)
+        @pl.loop(lo, hi, unroll=8)
         def _(i):
             s = (
                 lax.dot_general(q_ref[i], ck[i], NT, preferred_element_type=F32) * scale
@@ -333,23 +342,23 @@
         ].astype(BF16)
     x = xall[...]
     group = 8
-    part[...] = jnp.zeros(part.shape, F32)
-
-    @pl.loop(0, pool // group)
-    def _(g):
-        base = g * group
+    picked = jnp.zeros((rank, ntot), F32)
+    for base in range(0, pool, group):
         block = lax.dot_general(
-            pa[pl.ds(pl.multiple_of(base * rank, group * rank), group * rank), :],
+            pa[base * rank : (base + group) * rank, :],
             x,
             NT,
             preferred_element_type=F32,
         )
-        picked = jnp.zeros((rank, ntot), F32)
         for s in range(group):
             picked += jnp.where(
                 slot_row == base + s, block[s * rank : (s + 1) * rank], 0.0
             )
-        part[:, :, pl.ds(0, ntot)] += picked.reshape(nt, kpart, ntot)
+    if ntot_pad > ntot:
+        picked = jnp.concatenate(
+            [picked, jnp.zeros((rank, ntot_pad - ntot), F32)], axis=1
+        )
+    part[...] = picked.reshape(nt, kpart, ntot_pad)
 
     @pl.loop(1, nt)
     def _(k):
@@ -421,18 +430,14 @@
             axis=1,
         ).astype(BF16)
         w = wbuf[pl.ds(pl.multiple_of(source * width, width), width), :]
-        product = jnp.dot(normed, w, preferred_element_type=F32)
-        if o == 0:
-            acc_kv[...] = product
-        else:
-            acc_kv[...] += product
+        return jnp.dot(normed, w, preferred_element_type=F32)
 
     loads[2].wait()
     loads[3].wait()
-    project(0)
-    project(nt - 1)
+    first = project(0) + project(nt - 1)
     if half > 1:
-        project(1)
+        first += project(1)
+    acc_kv[...] = first
 
     length_row = len_ref[...].astype(F32)
     positions = jnp.sum(
@@ -449,8 +454,7 @@
 
     for h in range(3, half):
         ring_stage(h)
-        project(nt - h + 1)
-        project(h - 1)
+        acc_kv[...] += project(nt - h + 1) + project(h - 1)
 
     wait_bytes(coeff.at[pl.ds(0, nt - 1)], ag_recv)
     coeffs = coeff[...].reshape(rank, coeff.shape[2])[:, 0:ntot]
@@ -476,17 +480,16 @@
 
     loads[5].wait()
 
-    @pl.loop(0, rows, unroll=4)
+    @pl.loop(0, rows, unroll=8)
     def _(i):
         att_acc[pl.ds(pl.multiple_of(i * per_row, per_row), per_row), :] = jnp.dot(
             weights[i], cv[i], preferred_element_type=F32
         )
 
     if half > 2:
-        project(nt - half + 1)
-        project(half - 1)
+        acc_kv[...] += project(nt - half + 1) + project(half - 1)
     ring_stage(half)
-    project(half)
+    acc_kv[...] += project(half)
 
     key = acc_kv[:, 0:HD]
     turned = key * cos_ref[...] + pltpu.roll(key, HD // 2, 1) * sin_ref[...]

time: 39 us -> 38.4 us (0.985)
  Pallas kernels: 38.3 us -> 37.7 us
    pallas_call x1, Pallas kernels: 36.7 us -> 36.1 us  [shards(): pl.pallas_call(functools.partial(kernel, nr, nt), out_shape=(jax.ShapeDty...]
where the time goes in v8:
time: 38.4 us; the launch traced here: 38.3 us
  Pallas kernels  37.7 us (98%)
  between operations  0.64 us (2%)
    pallas_call x1, Pallas kernels, shards(): pl.pallas_call(functools.partial(kernel, nr, nt), out_shape=(jax.ShapeDty...  36.1 us
    pallas_call x1, Pallas kernels, shards(): pl.pallas_call(write_out, out_shape=shapes, in_specs=[vmem] * 3, out_spec...  1.61 us

profile of v8, /device:TPU:1, one launch (start us, length us, event | category | flops | bytes accessed | tf_op | source)
XLA Modules:
  0.0 38.3 jit_solution(12757470752558800096)
XLA Ops:
  0.6 36.1 %shard_map.157 = (bf16[64,1024]{1,0:T(8,128)(2,1)}, bf16[64,128]{1,0:T(8,128)(2,1)}, bf16[64,128]{1,0:T(8,128)(2,1)}) custom-call(bf16[64,1024]{1,0:T(8,128)(2,1)} %bitcast.16, bf16[8,128]{1,0:T(8,128)(2,1)} %bitcast.20, s32[1,1024]{1,0:T(1,128)} %bitcast.19, s32[16,32]{1,0:T(8,128)} %bitcast.18, s32[1,32]{1,0:T(1,128)} %bitcast.22, s32[32]{0:T(128)} %len_s_hbm.1, ...), custom_call_target="tpu_custom_call" | custom-call | flops 268435456 | bytes 12582912 | tf_op jit(solution)/shard_map/pallas_call | solution.py:596
  36.7 1.6 %shard_map.158 = (bf16[64,1024]{1,0:T(8,128)(2,1)}, bf16[64,128]{1,0:T(8,128)(2,1)}, bf16[64,128]{1,0:T(8,128)(2,1)}) custom-call(bf16[64,1024]{1,0:T(8,128)(2,1)} %get-tuple-element.9.a, bf16[64,128]{1,0:T(8,128)(2,1)} %get-tuple-element.10.b, bf16[64,128]{1,0:T(8,128)(2,1)} %get-tuple-element.11.c), custom_call_target="tpu_custom_call" | custom-call | tf_op jit(solution)/shard_map/pallas_call | solution.py:683

commit v9 on v8

--- a/solution.py
+++ b/solution.py
@@ -69,9 +69,8 @@
     got,
     xall,
     ring,
-    part,
-    rs_got,
-    coeff,
+    visit_part,
+    own_part,
     expand,
     ret_send,
     ret_got,
@@ -106,11 +105,9 @@
     need_count = need_ref.shape[0]
     adapters = place_ref.shape[1]
     pool = adapters // nr
-    rank = part.shape[1] * nt
-    kpart = rank // nt
+    rank = visit_part.shape[1]
     nvis = nr * 4
     ntot = nvis + rows2
-    ntot_pad = part.shape[2]
 
     small = [
         pltpu.make_async_copy(a, b, small_sem.at[k])
@@ -296,7 +293,8 @@
         visit.astype(BF16), spread.astype(BF16), preferred_element_type=F32
     )[0:1].astype(jnp.int32) - 1
     own_slot = jnp.where(is_far, -1, ra - need_count)
-    slot_row = jnp.concatenate([visit_slot, own_slot, own_slot], axis=1)
+    own_slot = jnp.concatenate([own_slot, own_slot], axis=1)
+    slot_row = jnp.concatenate([visit_slot, own_slot], axis=1)
 
     scale = 1.0 / math.sqrt(HD)
     cache_len = ck.shape[1]
@@ -333,6 +331,8 @@
     cached_scores(rows // 4, rows // 2)
     ring_stage(1, (1,))
 
+    loads[4].wait()
+    pbt[...] = pb[...].T
     loads[1].wait()
     wait_bytes(got.at[pl.ds(0, (nr - 1) * SENT), :], a2a_recv)
     wide_rows[...] = got[...].astype(F32)
@@ -354,23 +354,23 @@
             picked += jnp.where(
                 slot_row == base + s, block[s * rank : (s + 1) * rank], 0.0
             )
-    if ntot_pad > ntot:
-        picked = jnp.concatenate(
-            [picked, jnp.zeros((rank, ntot_pad - ntot), F32)], axis=1
-        )
-    part[...] = picked.reshape(nt, kpart, ntot_pad)
-
-    @pl.loop(1, nt)
-    def _(k):
-        to = lax.rem(t + k, nt)
-        pltpu.make_async_remote_copy(
-            src_ref=part.at[to],
-            dst_ref=rs_got.at[t],
-            send_sem=rs_send,
-            recv_sem=rs_recv,
-            device_id=(r, to),
-            device_id_type=MESH,
-        ).start()
+    visit_part[t] = picked[:, 0:nvis].astype(BF16)
+    own_part[t] = picked[:, nvis:ntot].astype(BF16)
+
+    def hand_round(ref, send_sem, recv_sem):
+        @pl.loop(1, nt)
+        def _(k):
+            pltpu.make_async_remote_copy(
+                src_ref=ref.at[t],
+                dst_ref=ref.at[t],
+                send_sem=send_sem,
+                recv_sem=recv_sem,
+                device_id=(r, lax.rem(t + k, nt)),
+                device_id_type=MESH,
+            ).start()
+
+    hand_round(visit_part, rs_send, rs_recv)
+    hand_round(own_part, ag_send, ag_recv)
 
     if half > 2:
         ring_stage(2, (0,))
@@ -393,20 +393,32 @@
     if half > 2:
         ring_stage(2, (1,))
 
-    wait_bytes(rs_got.at[pl.ds(0, nt - 1)], rs_recv)
-    whole = part[t]
-    for k in range(nt):
-        whole += jnp.where(k == t, 0.0, rs_got[k])
-    coeff[t] = whole
-
-    @pl.loop(1, nt)
+    def low_rank_terms(part, slots):
+        total = part[0].astype(F32)
+        for k in range(1, nt):
+            total += part[k].astype(F32)
+        coeffs = total.astype(BF16).astype(F32)
+        count = slots.shape[1]
+        for s in range(pool):
+            expand[s * rank : (s + 1) * rank, 0:count] = jnp.where(
+                slots == s, coeffs, 0.0
+            ).astype(BF16)
+        return jnp.dot(
+            pbt[...], expand[:, 0:count], preferred_element_type=F32
+        ).T
+
+    wait_bytes(visit_part.at[pl.ds(0, nt - 1)], rs_recv)
+    ret_send[...] = low_rank_terms(visit_part, visit_slot)
+
+    @pl.loop(1, nr)
     def _(k):
+        to = lax.rem(r + k, nr)
         pltpu.make_async_remote_copy(
-            src_ref=coeff.at[t],
-            dst_ref=coeff.at[t],
-            send_sem=ag_send,
-            recv_sem=ag_recv,
-            device_id=(r, lax.rem(t + k, nt)),
+            src_ref=ret_send.at[pl.ds(pl.multiple_of(to // 2 * 8, 8), 8), :],
+            dst_ref=ret_got.at[pl.ds(pl.multiple_of(r * 8, 8), 8), :],
+            send_sem=re_send,
+            recv_sem=re_recv,
+            device_id=(to, t),
             device_id_type=MESH,
         ).start()
 
@@ -449,34 +461,9 @@
     cos_ref[...] = jnp.cos(angle)
     sin_ref[...] = jnp.sin(angle) * sign
 
-    loads[4].wait()
-    pbt[...] = pb[...].T
-
     for h in range(3, half):
         ring_stage(h)
         acc_kv[...] += project(nt - h + 1) + project(h - 1)
-
-    wait_bytes(coeff.at[pl.ds(0, nt - 1)], ag_recv)
-    coeffs = coeff[...].reshape(rank, coeff.shape[2])[:, 0:ntot]
-    for s in range(pool):
-        expand[s * rank : (s + 1) * rank, :] = jnp.where(
-            slot_row == s, coeffs, 0.0
-        ).astype(BF16)
-    delta = jnp.dot(pbt[...], expand[...], preferred_element_type=F32).T
-    ret_send[...] = delta[0:nvis]
-    own_delta = delta[nvis:ntot]
-
-    @pl.loop(1, nr)
-    def _(k):
-        to = lax.rem(r + k, nr)
-        pltpu.make_async_remote_copy(
-            src_ref=ret_send.at[pl.ds(pl.multiple_of(to // 2 * 8, 8), 8), :],
-            dst_ref=ret_got.at[pl.ds(pl.multiple_of(r * 8, 8), 8), :],
-            send_sem=re_send,
-            recv_sem=re_recv,
-            device_id=(to, t),
-            device_id_type=MESH,
-        ).start()
 
     loads[5].wait()
 
@@ -518,6 +505,8 @@
         fresh_w[part_rows, :] = (e_fresh * share).astype(BF16)
         att_acc[part_rows, :] = att_acc[part_rows, :] * (shrink * share)
 
+    wait_bytes(own_part.at[pl.ds(0, nt - 1)], ag_recv)
+    own_delta = low_rank_terms(own_part, own_slot)
     code_f = jnp.where(
         is_far, owner * 8 + lax.rem(r, 2) * 4 + turn * 2, -1000
     ).astype(F32)
@@ -547,8 +536,8 @@
             hop(way, h, c).wait_send()
     wait_bytes(stats.at[pl.ds(0, nt - 1)], st_send)
     wait_bytes(msg.at[pl.ds(0, (nr - 1) * SENT), :], a2a_send)
-    wait_bytes(part.at[pl.ds(0, nt - 1)], rs_send)
-    wait_bytes(coeff.at[pl.ds(0, nt - 1)], ag_send)
+    wait_bytes(visit_part.at[pl.ds(0, nt - 1)], rs_send)
+    wait_bytes(own_part.at[pl.ds(0, nt - 1)], ag_send)
     wait_bytes(ret_got.at[pl.ds(0, (nr - 1) * 8), :], re_send)
 
 
@@ -585,7 +574,6 @@
     rows2 = steps * rows
     nvis = nr * 4
     ntot = nvis + rows2
-    ntot_pad = -(-ntot // HD) * HD
     per_row = steps * GROUP
     half = HD // 2
     frequency = np.float32(THETA) ** (-(np.arange(half, dtype=np.float32) * 2.0) / HD)
@@ -626,10 +614,9 @@
             pltpu.VMEM((nr * SENT, HD), BF16),
             pltpu.VMEM((ntot, width), BF16),
             pltpu.VMEM((nt, rows2, width), BF16),
-            pltpu.VMEM((nt, rank // nt, ntot_pad), F32),
-            pltpu.VMEM((nt, rank // nt, ntot_pad), F32),
-            pltpu.VMEM((nt, rank // nt, ntot_pad), F32),
-            pltpu.VMEM((pool * rank, ntot), BF16),
+            pltpu.VMEM((nt, rank, nvis), BF16),
+            pltpu.VMEM((nt, rank, rows2), BF16),
+            pltpu.VMEM((pool * rank, nvis), BF16),
             pltpu.VMEM((nvis, HD), F32),
             pltpu.VMEM((nr * 8, HD), F32),
             pltpu.VMEM((rows, per_row, cache_len), F32),

time: 38.4 us -> 36.8 us (0.958)
  Pallas kernels: 37.7 us -> 36 us
    pallas_call x1, Pallas kernels: 36.1 us -> 34.4 us  [shards(): pl.pallas_call(functools.partial(kernel, nr, nt), out_shape=(jax.ShapeDty...]
where the time goes in v9:
time: 36.8 us; the launch traced here: 36.7 us
  Pallas kernels  36 us (98%)
  between operations  0.64 us (2%)
    pallas_call x1, Pallas kernels, shards(): pl.pallas_call(functools.partial(kernel, nr, nt), out_shape=(jax.ShapeDty...  34.4 us
    pallas_call x1, Pallas kernels, shards(): pl.pallas_call(write_out, out_shape=shapes, in_specs=[vmem] * 3, out_spec...  1.61 us

profile of v9, /device:TPU:1, one launch (start us, length us, event | category | flops | bytes accessed | tf_op | source)
XLA Modules:
  0.0 36.7 jit_solution(11941939061577936235)
XLA Ops:
  0.6 34.4 %shard_map.157 = (bf16[64,1024]{1,0:T(8,128)(2,1)}, bf16[64,128]{1,0:T(8,128)(2,1)}, bf16[64,128]{1,0:T(8,128)(2,1)}) custom-call(bf16[64,1024]{1,0:T(8,128)(2,1)} %bitcast.16, bf16[8,128]{1,0:T(8,128)(2,1)} %bitcast.20, s32[1,1024]{1,0:T(1,128)} %bitcast.19, s32[16,32]{1,0:T(8,128)} %bitcast.18, s32[1,32]{1,0:T(1,128)} %bitcast.22, s32[32]{0:T(128)} %len_s_hbm.1, ...), custom_call_target="tpu_custom_call" | custom-call | flops 268435456 | bytes 12582912 | tf_op jit(solution)/shard_map/pallas_call | solution.py:584
  35.1 1.6 %shard_map.158 = (bf16[64,1024]{1,0:T(8,128)(2,1)}, bf16[64,128]{1,0:T(8,128)(2,1)}, bf16[64,128]{1,0:T(8,128)(2,1)}) custom-call(bf16[64,1024]{1,0:T(8,128)(2,1)} %get-tuple-element.9.a, bf16[64,128]{1,0:T(8,128)(2,1)} %get-tuple-element.10.b, bf16[64,128]{1,0:T(8,128)(2,1)} %get-tuple-element.11.c), custom_call_target="tpu_custom_call" | custom-call | tf_op jit(solution)/shard_map/pallas_call | solution.py:670

commit v10 on v9

--- a/solution.py
+++ b/solution.py
@@ -330,6 +330,18 @@
     ring_stage(1, (0,))
     cached_scores(rows // 4, rows // 2)
     ring_stage(1, (1,))
+    cached_scores(rows // 2, rows)
+
+    length_row = len_ref[...].astype(F32)
+    positions = jnp.sum(
+        jnp.where(eye_r, length_row, 0.0), axis=1, keepdims=True
+    )
+    positions = jnp.concatenate([positions, positions + 1.0], axis=0)
+    angle = positions * freq_ref[...]
+    sign = jnp.where(iota((rows2, HD), 1) < HD // 2, -1.0, 1.0)
+    cos_ref[...] = jnp.cos(angle)
+    sin_ref[...] = jnp.sin(angle) * sign
+
 
     loads[4].wait()
     pbt[...] = pb[...].T
@@ -374,7 +386,6 @@
 
     if half > 2:
         ring_stage(2, (0,))
-    cached_scores(rows // 2, rows)
 
     qrows = 8
     span = qrows * per_row
@@ -392,35 +403,6 @@
 
     if half > 2:
         ring_stage(2, (1,))
-
-    def low_rank_terms(part, slots):
-        total = part[0].astype(F32)
-        for k in range(1, nt):
-            total += part[k].astype(F32)
-        coeffs = total.astype(BF16).astype(F32)
-        count = slots.shape[1]
-        for s in range(pool):
-            expand[s * rank : (s + 1) * rank, 0:count] = jnp.where(
-                slots == s, coeffs, 0.0
-            ).astype(BF16)
-        return jnp.dot(
-            pbt[...], expand[:, 0:count], preferred_element_type=F32
-        ).T
-
-    wait_bytes(visit_part.at[pl.ds(0, nt - 1)], rs_recv)
-    ret_send[...] = low_rank_terms(visit_part, visit_slot)
-
-    @pl.loop(1, nr)
-    def _(k):
-        to = lax.rem(r + k, nr)
-        pltpu.make_async_remote_copy(
-            src_ref=ret_send.at[pl.ds(pl.multiple_of(to // 2 * 8, 8), 8), :],
-            dst_ref=ret_got.at[pl.ds(pl.multiple_of(r * 8, 8), 8), :],
-            send_sem=re_send,
-            recv_sem=re_recv,
-            device_id=(to, t),
-            device_id_type=MESH,
-        ).start()
 
     wait_bytes(stats.at[pl.ds(0, nt - 1)], st_recv)
     square = stats[0, 8:16, :]
@@ -451,20 +433,6 @@
         first += project(1)
     acc_kv[...] = first
 
-    length_row = len_ref[...].astype(F32)
-    positions = jnp.sum(
-        jnp.where(eye_r, length_row, 0.0), axis=1, keepdims=True
-    )
-    positions = jnp.concatenate([positions, positions + 1.0], axis=0)
-    angle = positions * freq_ref[...]
-    sign = jnp.where(iota((rows2, HD), 1) < HD // 2, -1.0, 1.0)
-    cos_ref[...] = jnp.cos(angle)
-    sin_ref[...] = jnp.sin(angle) * sign
-
-    for h in range(3, half):
-        ring_stage(h)
-        acc_kv[...] += project(nt - h + 1) + project(h - 1)
-
     loads[5].wait()
 
     @pl.loop(0, rows, unroll=8)
@@ -473,6 +441,43 @@
             weights[i], cv[i], preferred_element_type=F32
         )
 
+    for h in range(3, half):
+        ring_stage(h, (0,))
+
+    def low_rank_terms(part, slots):
+        total = part[0].astype(F32)
+        for k in range(1, nt):
+            total += part[k].astype(F32)
+        coeffs = total.astype(BF16).astype(F32)
+        count = slots.shape[1]
+        for s in range(pool):
+            expand[s * rank : (s + 1) * rank, 0:count] = jnp.where(
+                slots == s, coeffs, 0.0
+            ).astype(BF16)
+        return jnp.dot(
+            pbt[...], expand[:, 0:count], preferred_element_type=F32
+        ).T
+
+    wait_bytes(visit_part.at[pl.ds(0, nt - 1)], rs_recv)
+    ret_send[...] = low_rank_terms(visit_part, visit_slot)
+
+    @pl.loop(1, nr)
+    def _(k):
+        to = lax.rem(r + k, nr)
+        pltpu.make_async_remote_copy(
+            src_ref=ret_send.at[pl.ds(pl.multiple_of(to // 2 * 8, 8), 8), :],
+            dst_ref=ret_got.at[pl.ds(pl.multiple_of(r * 8, 8), 8), :],
+            send_sem=re_send,
+            recv_sem=re_recv,
+            device_id=(to, t),
+            device_id_type=MESH,
+        ).start()
+
+    for h in range(3, half):
+        ring_stage(h, (1,))
+        acc_kv[...] += project(nt - h + 1) + project(h - 1)
+    wait_bytes(own_part.at[pl.ds(0, nt - 1)], ag_recv)
+    own_delta = low_rank_terms(own_part, own_slot)
     if half > 2:
         acc_kv[...] += project(nt - half + 1) + project(half - 1)
     ring_stage(half)
@@ -505,8 +510,6 @@
         fresh_w[part_rows, :] = (e_fresh * share).astype(BF16)
         att_acc[part_rows, :] = att_acc[part_rows, :] * (shrink * share)
 
-    wait_bytes(own_part.at[pl.ds(0, nt - 1)], ag_recv)
-    own_delta = low_rank_terms(own_part, own_slot)
     code_f = jnp.where(
         is_far, owner * 8 + lax.rem(r, 2) * 4 + turn * 2, -1000
     ).astype(F32)

time: 36.8 us -> 39.1 us (1.063)
  Pallas kernels: 36 us -> 38.3 us
    pallas_call x1, Pallas kernels: 34.4 us -> 36.7 us  [shards(): pl.pallas_call(functools.partial(kernel, nr, nt), out_shape=(jax.ShapeDty...]
where the time goes in v10:
time: 39.1 us; the launch traced here: 39 us
  Pallas kernels  38.3 us (98%)
  between operations  0.64 us (2%)
    pallas_call x1, Pallas kernels, shards(): pl.pallas_call(functools.partial(kernel, nr, nt), out_shape=(jax.ShapeDty...  36.7 us
    pallas_call x1, Pallas kernels, shards(): pl.pallas_call(write_out, out_shape=shapes, in_specs=[vmem] * 3, out_spec...  1.61 us

profile of v10, /device:TPU:1, one launch (start us, length us, event | category | flops | bytes accessed | tf_op | source)
XLA Modules:
  0.0 39.0 jit_solution(14603643912720380848)
XLA Ops:
  0.6 36.7 %shard_map.157 = (bf16[64,1024]{1,0:T(8,128)(2,1)}, bf16[64,128]{1,0:T(8,128)(2,1)}, bf16[64,128]{1,0:T(8,128)(2,1)}) custom-call(bf16[64,1024]{1,0:T(8,128)(2,1)} %bitcast.16, bf16[8,128]{1,0:T(8,128)(2,1)} %bitcast.20, s32[1,1024]{1,0:T(1,128)} %bitcast.19, s32[16,32]{1,0:T(8,128)} %bitcast.18, s32[1,32]{1,0:T(1,128)} %bitcast.22, s32[32]{0:T(128)} %len_s_hbm.1, ...), custom_call_target="tpu_custom_call" | custom-call | flops 268435456 | bytes 12582912 | tf_op jit(solution)/shard_map/pallas_call | solution.py:587
  37.4 1.6 %shard_map.158 = (bf16[64,1024]{1,0:T(8,128)(2,1)}, bf16[64,128]{1,0:T(8,128)(2,1)}, bf16[64,128]{1,0:T(8,128)(2,1)}) custom-call(bf16[64,1024]{1,0:T(8,128)(2,1)} %get-tuple-element.9.a, bf16[64,128]{1,0:T(8,128)(2,1)} %get-tuple-element.10.b, bf16[64,128]{1,0:T(8,128)(2,1)} %get-tuple-element.11.c), custom_call_target="tpu_custom_call" | custom-call | tf_op jit(solution)/shard_map/pallas_call | solution.py:673

commit v11 on v9

--- a/solution.py
+++ b/solution.py
@@ -328,11 +328,8 @@
     loads[0].wait()
     cached_scores(0, rows // 4)
     ring_stage(1, (0,))
-    cached_scores(rows // 4, rows // 2)
     ring_stage(1, (1,))
 
-    loads[4].wait()
-    pbt[...] = pb[...].T
     loads[1].wait()
     wait_bytes(got.at[pl.ds(0, (nr - 1) * SENT), :], a2a_recv)
     wide_rows[...] = got[...].astype(F32)
@@ -374,22 +371,9 @@
 
     if half > 2:
         ring_stage(2, (0,))
-    cached_scores(rows // 2, rows)
-
-    qrows = 8
-    span = qrows * per_row
-    for b in range(rows // qrows):
-        s = scores[b * qrows : (b + 1) * qrows].reshape(span, cache_len)
-        top = jnp.max(s, axis=1, keepdims=True)
-        e_cache = jnp.exp(s - top)
-        top_ref[b * span : (b + 1) * span, :] = top
-        bottom_ref[b * span : (b + 1) * span, :] = jnp.sum(
-            e_cache, axis=1, keepdims=True
-        )
-        weights[b * qrows : (b + 1) * qrows] = e_cache.astype(BF16).reshape(
-            qrows, per_row, cache_len
-        )
-
+    cached_scores(rows // 4, rows // 2)
+    loads[4].wait()
+    pbt[...] = pb[...].T
     if half > 2:
         ring_stage(2, (1,))
 
@@ -421,6 +405,24 @@
             device_id=(to, t),
             device_id_type=MESH,
         ).start()
+
+    cached_scores(rows // 2, rows)
+    for h in range(3, half):
+        ring_stage(h)
+
+    qrows = 8
+    span = qrows * per_row
+    for b in range(rows // qrows):
+        s = scores[b * qrows : (b + 1) * qrows].reshape(span, cache_len)
+        top = jnp.max(s, axis=1, keepdims=True)
+        e_cache = jnp.exp(s - top)
+        top_ref[b * span : (b + 1) * span, :] = top
+        bottom_ref[b * span : (b + 1) * span, :] = jnp.sum(
+            e_cache, axis=1, keepdims=True
+        )
+        weights[b * qrows : (b + 1) * qrows] = e_cache.astype(BF16).reshape(
+            qrows, per_row, cache_len
+        )
 
     wait_bytes(stats.at[pl.ds(0, nt - 1)], st_recv)
     square = stats[0, 8:16, :]
@@ -462,7 +464,6 @@
     sin_ref[...] = jnp.sin(angle) * sign
 
     for h in range(3, half):
-        ring_stage(h)
         acc_kv[...] += project(nt - h + 1) + project(h - 1)
 
     loads[5].wait()
@@ -473,6 +474,8 @@
             weights[i], cv[i], preferred_element_type=F32
         )
 
+    wait_bytes(own_part.at[pl.ds(0, nt - 1)], ag_recv)
+    own_delta = low_rank_terms(own_part, own_slot)
     if half > 2:
         acc_kv[...] += project(nt - half + 1) + project(half - 1)
     ring_stage(half)
@@ -505,8 +508,6 @@
         fresh_w[part_rows, :] = (e_fresh * share).astype(BF16)
         att_acc[part_rows, :] = att_acc[part_rows, :] * (shrink * share)
 
-    wait_bytes(own_part.at[pl.ds(0, nt - 1)], ag_recv)
-    own_delta = low_rank_terms(own_part, own_slot)
     code_f = jnp.where(
         is_far, owner * 8 + lax.rem(r, 2) * 4 + turn * 2, -1000
     ).astype(F32)

time: 36.8 us -> 36.3 us (0.986)
  Pallas kernels: 36 us -> 35.6 us
    pallas_call x1, Pallas kernels: 34.4 us -> 33.9 us  [shards(): pl.pallas_call(functools.partial(kernel, nr, nt), out_shape=(jax.ShapeDty...]
where the time goes in v11:
time: 36.3 us; the launch traced here: 36.2 us
  Pallas kernels  35.6 us (98%)
  between operations  0.64 us (2%)
    pallas_call x1, Pallas kernels, shards(): pl.pallas_call(functools.partial(kernel, nr, nt), out_shape=(jax.ShapeDty...  33.9 us
    pallas_call x1, Pallas kernels, shards(): pl.pallas_call(write_out, out_shape=shapes, in_specs=[vmem] * 3, out_spec...  1.61 us

profile of v11, /device:TPU:1, one launch (start us, length us, event | category | flops | bytes accessed | tf_op | source)
XLA Modules:
  0.0 36.2 jit_solution(2058777903596275094)
XLA Ops:
  0.6 33.9 %shard_map.157 = (bf16[64,1024]{1,0:T(8,128)(2,1)}, bf16[64,128]{1,0:T(8,128)(2,1)}, bf16[64,128]{1,0:T(8,128)(2,1)}) custom-call(bf16[64,1024]{1,0:T(8,128)(2,1)} %bitcast.16, bf16[8,128]{1,0:T(8,128)(2,1)} %bitcast.20, s32[1,1024]{1,0:T(1,128)} %bitcast.19, s32[16,32]{1,0:T(8,128)} %bitcast.18, s32[1,32]{1,0:T(1,128)} %bitcast.22, s32[32]{0:T(128)} %len_s_hbm.1, ...), custom_call_target="tpu_custom_call" | custom-call | flops 268435456 | bytes 12582912 | tf_op jit(solution)/shard_map/pallas_call | solution.py:585
  34.6 1.6 %shard_map.158 = (bf16[64,1024]{1,0:T(8,128)(2,1)}, bf16[64,128]{1,0:T(8,128)(2,1)}, bf16[64,128]{1,0:T(8,128)(2,1)}) custom-call(bf16[64,1024]{1,0:T(8,128)(2,1)} %get-tuple-element.9.a, bf16[64,128]{1,0:T(8,128)(2,1)} %get-tuple-element.10.b, bf16[64,128]{1,0:T(8,128)(2,1)} %get-tuple-element.11.c), custom_call_target="tpu_custom_call" | custom-call | tf_op jit(solution)/shard_map/pallas_call | solution.py:671

commit v12 on v11

--- a/solution.py
+++ b/solution.py
@@ -138,7 +138,7 @@
 
     barrier = pltpu.get_barrier_semaphore()
 
-    @pl.loop(1, nr)
+    @pl.loop(1, nr, unroll=True)
     def _(k):
         pl.semaphore_signal(
             barrier, inc=1, device_id=(lax.rem(r + k, nr), t), device_id_type=MESH
@@ -247,7 +247,7 @@
     got[pl.ds(pl.multiple_of(r * SENT, SENT), SENT), :] = jnp.zeros((SENT, HD), BF16)
     ret_got[pl.ds(pl.multiple_of(r * 8, 8), 8), :] = jnp.zeros((8, HD), F32)
 
-    @pl.loop(1, nr)
+    @pl.loop(1, nr, unroll=True)
     def _(k):
         to = lax.rem(r + k, nr)
         pltpu.make_async_remote_copy(
@@ -355,7 +355,7 @@
     own_part[t] = picked[:, nvis:ntot].astype(BF16)
 
     def hand_round(ref, send_sem, recv_sem):
-        @pl.loop(1, nt)
+        @pl.loop(1, nt, unroll=True)
         def _(k):
             pltpu.make_async_remote_copy(
                 src_ref=ref.at[t],
@@ -394,7 +394,7 @@
     wait_bytes(visit_part.at[pl.ds(0, nt - 1)], rs_recv)
     ret_send[...] = low_rank_terms(visit_part, visit_slot)
 
-    @pl.loop(1, nr)
+    @pl.loop(1, nr, unroll=True)
     def _(k):
         to = lax.rem(r + k, nr)
         pltpu.make_async_remote_copy(
@@ -457,11 +457,16 @@
     positions = jnp.sum(
         jnp.where(eye_r, length_row, 0.0), axis=1, keepdims=True
     )
-    positions = jnp.concatenate([positions, positions + 1.0], axis=0)
-    angle = positions * freq_ref[...]
-    sign = jnp.where(iota((rows2, HD), 1) < HD // 2, -1.0, 1.0)
-    cos_ref[...] = jnp.cos(angle)
-    sin_ref[...] = jnp.sin(angle) * sign
+    front = iota((rows, HD), 1) < HD // 2
+    angle = (positions + jnp.where(front, 0.0, 1.0)) * freq_ref[...]
+    cosine = jnp.cos(angle)
+    sine = jnp.sin(angle)
+    cosine_turned = pltpu.roll(cosine, HD // 2, 1)
+    sine_turned = pltpu.roll(sine, HD // 2, 1)
+    cos_ref[0:rows, :] = jnp.where(front, cosine, cosine_turned)
+    cos_ref[rows:rows2, :] = jnp.where(front, cosine_turned, cosine)
+    sin_ref[0:rows, :] = jnp.where(front, -sine, sine_turned)
+    sin_ref[rows:rows2, :] = jnp.where(front, -sine_turned, sine)
 
     for h in range(3, half):
         acc_kv[...] += project(nt - h + 1) + project(h - 1)

time: 36.3 us -> 36.3 us (level)
  no operation moved by 1% of the time
where the time goes in v12:
time: 36.3 us; the launch traced here: 36.1 us
  Pallas kernels  35.5 us (98%)
  between operations  0.64 us (2%)
    pallas_call x1, Pallas kernels, shards(): pl.pallas_call(functools.partial(kernel, nr, nt), out_shape=(jax.ShapeDty...  33.9 us
    pallas_call x1, Pallas kernels, shards(): pl.pallas_call(write_out, out_shape=shapes, in_specs=[vmem] * 3, out_spec...  1.61 us

profile of v12, /device:TPU:1, one launch (start us, length us, event | category | flops | bytes accessed | tf_op | source)
XLA Modules:
  0.0 36.1 jit_solution(6764025504951012658)
XLA Ops:
  0.6 33.9 %shard_map.157 = (bf16[64,1024]{1,0:T(8,128)(2,1)}, bf16[64,128]{1,0:T(8,128)(2,1)}, bf16[64,128]{1,0:T(8,128)(2,1)}) custom-call(bf16[64,1024]{1,0:T(8,128)(2,1)} %bitcast.16, bf16[8,128]{1,0:T(8,128)(2,1)} %bitcast.20, s32[1,1024]{1,0:T(1,128)} %bitcast.19, s32[16,32]{1,0:T(8,128)} %bitcast.18, s32[1,32]{1,0:T(1,128)} %bitcast.22, s32[32]{0:T(128)} %len_s_hbm.1, ...), custom_call_target="tpu_custom_call" | custom-call | flops 268435456 | bytes 12582912 | tf_op jit(solution)/shard_map/pallas_call | solution.py:590
  34.5 1.6 %shard_map.158 = (bf16[64,1024]{1,0:T(8,128)(2,1)}, bf16[64,128]{1,0:T(8,128)(2,1)}, bf16[64,128]{1,0:T(8,128)(2,1)}) custom-call(bf16[64,1024]{1,0:T(8,128)(2,1)} %get-tuple-element.9.a, bf16[64,128]{1,0:T(8,128)(2,1)} %get-tuple-element.10.b, bf16[64,128]{1,0:T(8,128)(2,1)} %get-tuple-element.11.c), custom_call_target="tpu_custom_call" | custom-call | tf_op jit(solution)/shard_map/pallas_call | solution.py:676

commit v13 on v12

--- a/solution.py
+++ b/solution.py
@@ -317,16 +317,6 @@
             if (way, c) in (hops(h + 1) if h < half else []):
                 hop(way, h + 1, c).start()
 
-    for load in small[5:]:
-        load.wait()
-    for step in range(2):
-        for g in range(GROUP):
-            q_wide[pl.ds(step * GROUP + g, rows, stride=per_row), :] = q_in[
-                step * rows : (step + 1) * rows, g * HD : (g + 1) * HD
-            ].astype(F32)
-    q_ref[...] = q_wide[...].astype(BF16).reshape(rows, per_row, HD)
-    loads[0].wait()
-    cached_scores(0, rows // 4)
     ring_stage(1, (0,))
     ring_stage(1, (1,))
 
@@ -371,7 +361,16 @@
 
     if half > 2:
         ring_stage(2, (0,))
-    cached_scores(rows // 4, rows // 2)
+    for load in small[5:]:
+        load.wait()
+    for step in range(2):
+        for g in range(GROUP):
+            q_wide[pl.ds(step * GROUP + g, rows, stride=per_row), :] = q_in[
+                step * rows : (step + 1) * rows, g * HD : (g + 1) * HD
+            ].astype(F32)
+    q_ref[...] = q_wide[...].astype(BF16).reshape(rows, per_row, HD)
+    loads[0].wait()
+    cached_scores(0, rows // 2)
     loads[4].wait()
     pbt[...] = pb[...].T
     if half > 2:

time: 36.3 us -> 36.3 us (level)
  no operation moved by 1% of the time
where the time goes in v13:
time: 36.3 us; the launch traced here: 36.1 us
  Pallas kernels  35.5 us (98%)
  between operations  0.64 us (2%)
    pallas_call x1, Pallas kernels, shards(): pl.pallas_call(functools.partial(kernel, nr, nt), out_shape=(jax.ShapeDty...  33.9 us
    pallas_call x1, Pallas kernels, shards(): pl.pallas_call(write_out, out_shape=shapes, in_specs=[vmem] * 3, out_spec...  1.61 us

profile of v13, /device:TPU:1, one launch (start us, length us, event | category | flops | bytes accessed | tf_op | source)
XLA Modules:
  0.0 36.1 jit_solution(13830131305435749236)
XLA Ops:
  0.6 33.9 %shard_map.157 = (bf16[64,1024]{1,0:T(8,128)(2,1)}, bf16[64,128]{1,0:T(8,128)(2,1)}, bf16[64,128]{1,0:T(8,128)(2,1)}) custom-call(bf16[64,1024]{1,0:T(8,128)(2,1)} %bitcast.16, bf16[8,128]{1,0:T(8,128)(2,1)} %bitcast.20, s32[1,1024]{1,0:T(1,128)} %bitcast.19, s32[16,32]{1,0:T(8,128)} %bitcast.18, s32[1,32]{1,0:T(1,128)} %bitcast.22, s32[32]{0:T(128)} %len_s_hbm.1, ...), custom_call_target="tpu_custom_call" | custom-call | flops 268435456 | bytes 12582912 | tf_op jit(solution)/shard_map/pallas_call | solution.py:589
  34.5 1.6 %shard_map.158 = (bf16[64,1024]{1,0:T(8,128)(2,1)}, bf16[64,128]{1,0:T(8,128)(2,1)}, bf16[64,128]{1,0:T(8,128)(2,1)}) custom-call(bf16[64,1024]{1,0:T(8,128)(2,1)} %get-tuple-element.9.a, bf16[64,128]{1,0:T(8,128)(2,1)} %get-tuple-element.10.b, bf16[64,128]{1,0:T(8,128)(2,1)} %get-tuple-element.11.c), custom_call_target="tpu_custom_call" | custom-call | tf_op jit(solution)/shard_map/pallas_call | solution.py:675

commit v14 on v13

--- a/solution.py
+++ b/solution.py
@@ -357,10 +357,10 @@
             ).start()
 
     hand_round(visit_part, rs_send, rs_recv)
-    hand_round(own_part, ag_send, ag_recv)
 
     if half > 2:
         ring_stage(2, (0,))
+    hand_round(own_part, ag_send, ag_recv)
     for load in small[5:]:
         load.wait()
     for step in range(2):
@@ -405,10 +405,10 @@
             device_id_type=MESH,
         ).start()
 
-    cached_scores(rows // 2, rows)
     for h in range(3, half):
         ring_stage(h)
 
+    cached_scores(rows // 2, rows)
     qrows = 8
     span = qrows * per_row
     for b in range(rows // qrows):

time: 36.3 us -> 36.9 us (1.017)
  Pallas kernels: 35.5 us -> 36.1 us
    pallas_call x1, Pallas kernels: 33.9 us -> 34.5 us  [shards(): pl.pallas_call(functools.partial(kernel, nr, nt), out_shape=(jax.ShapeDty...]
where the time goes in v14:
time: 36.9 us; the launch traced here: 36.8 us
  Pallas kernels  36.1 us (98%)
  between operations  0.64 us (2%)
    pallas_call x1, Pallas kernels, shards(): pl.pallas_call(functools.partial(kernel, nr, nt), out_shape=(jax.ShapeDty...  34.5 us
    pallas_call x1, Pallas kernels, shards(): pl.pallas_call(write_out, out_shape=shapes, in_specs=[vmem] * 3, out_spec...  1.61 us

profile of v14, /device:TPU:1, one launch (start us, length us, event | category | flops | bytes accessed | tf_op | source)
XLA Modules:
  0.0 36.8 jit_solution(9008720530470628562)
XLA Ops:
  0.6 34.5 %shard_map.157 = (bf16[64,1024]{1,0:T(8,128)(2,1)}, bf16[64,128]{1,0:T(8,128)(2,1)}, bf16[64,128]{1,0:T(8,128)(2,1)}) custom-call(bf16[64,1024]{1,0:T(8,128)(2,1)} %bitcast.16, bf16[8,128]{1,0:T(8,128)(2,1)} %bitcast.20, s32[1,1024]{1,0:T(1,128)} %bitcast.19, s32[16,32]{1,0:T(8,128)} %bitcast.18, s32[1,32]{1,0:T(1,128)} %bitcast.22, s32[32]{0:T(128)} %len_s_hbm.1, ...), custom_call_target="tpu_custom_call" | custom-call | flops 268435456 | bytes 12582912 | tf_op jit(solution)/shard_map/pallas_call | solution.py:589
  35.2 1.6 %shard_map.158 = (bf16[64,1024]{1,0:T(8,128)(2,1)}, bf16[64,128]{1,0:T(8,128)(2,1)}, bf16[64,128]{1,0:T(8,128)(2,1)}) custom-call(bf16[64,1024]{1,0:T(8,128)(2,1)} %get-tuple-element.9.a, bf16[64,128]{1,0:T(8,128)(2,1)} %get-tuple-element.10.b, bf16[64,128]{1,0:T(8,128)(2,1)} %get-tuple-element.11.c), custom_call_target="tpu_custom_call" | custom-call | tf_op jit(solution)/shard_map/pallas_call | solution.py:675
